TPU v7x, 256 devices: a whole 4x4x8 slice. The times are simulated.
256 devices in a mesh: seq: 64 (over z, x_hi, y), head: 4 (over x_lo, core).
Axes of the slice: x: 4 (x_hi: 2, x_lo: 2; x = x_hi * 2 + x_lo), y: 4, z: 8, core: 2. Of those that a mesh axis runs over, the one named last changes fastest.
Arguments:
- queries: bfloat16 [8192, 2560], P(('seq', 'head')), may hold values from -6 to 6
- keys: bfloat16 [8192, 2560], P(('seq', 'head')), may hold values from -6 to 6
- values: bfloat16 [8192, 2560], P(('seq', 'head')), may hold values from -6 to 6
- residual: bfloat16 [8192, 5120], P(('seq', 'head')), may hold values from -6 to 6
- cached_context: bfloat16 [8192, 2560], P('seq', 'head'), may hold values from -3 to 3
- out_weight_a: bfloat16 [2560, 5120], P('head'), may hold values from -0.125 to 0.125
- out_weight_b: bfloat16 [2560, 5120], P('head', 'seq'), may hold values from -0.125 to 0.125
- gate_a: float32 [5120], replicated, may hold values from 0.5 to 2
- gate_b: float32 [5120], replicated, may hold values from 0.5 to 2
Outputs:
- mixed: bfloat16 [8192, 5120], P(('seq', 'head'))
- attn_cache: bfloat16 [8192, 2560], P('seq', 'head')
All inputs are finite; a program needn't handle non-finite values.
Results may differ from a plain program's by a relative error of at most 0.013.
Values may be sent and summed in bfloat16 or wider, within the bound.
A program may use at most 128 MiB of HBM per device.

v0:
```python
import math

import jax
import jax.numpy as jnp
from jax import lax
from jax.sharding import PartitionSpec as P

HD = 128


def column_product(cached_context, out_weight_b):
    return jnp.dot(
        cached_context,
        lax.all_gather(out_weight_b, "seq", axis=1, tiled=True),
        preferred_element_type=jnp.float32,
    )


def on_device(
    queries, keys, values, residual, cached_context, out_weight_a, out_weight_b, gate_a, gate_b
):
    query_part, key_part, value_part = (
        lax.all_to_all(queries, "head", split_axis=1, concat_axis=0, tiled=True),
        lax.all_to_all(keys, "head", split_axis=1, concat_axis=0, tiled=True),
        lax.all_to_all(values, "head", split_axis=1, concat_axis=0, tiled=True),
    )
    row_count = query_part.shape[0]
    col_count = query_part.shape[1]
    head_count = col_count // HD
    score_scale = 1.0 / math.sqrt(HD)
    query_heads = query_part.reshape(row_count, head_count, HD)
    run_max = jnp.full((head_count, row_count), -1e30, jnp.float32)
    key_piece = lax.all_gather(key_part, "seq", axis=0, tiled=True)
    value_piece = lax.all_gather(value_part, "seq", axis=0, tiled=True)
    length = key_piece.shape[0]
    key_heads = key_piece.reshape(length, head_count, HD)
    value_heads = value_piece.reshape(length, head_count, HD)
    scores = (
        jnp.einsum("rhd,nhd->hrn", query_heads, key_heads, preferred_element_type=jnp.float32)
        * score_scale
    )
    new_max = jnp.maximum(run_max, jnp.max(scores, axis=2))
    weights = jnp.exp(scores - new_max[:, :, None])
    new_sum = jnp.sum(weights, axis=2)
    update = jnp.einsum(
        "hrn,nhd->hrd",
        weights.astype(jnp.bfloat16),
        value_heads,
        preferred_element_type=jnp.float32,
    )
    context = (update / new_sum[:, :, None]).astype(jnp.bfloat16)
    attn_cache = context.transpose(1, 0, 2).reshape(row_count, col_count)
    branch_b = column_product(cached_context, out_weight_b)
    first_rows = jnp.dot(attn_cache, out_weight_a, preferred_element_type=jnp.float32)
    summed = lax.psum_scatter(
        (gate_a * first_rows + gate_b * branch_b).astype(jnp.bfloat16),
        "head",
        scatter_dimension=0,
        tiled=True,
    ).astype(jnp.float32)
    mixed = (residual.astype(jnp.float32) + summed).astype(jnp.bfloat16)
    return (mixed, attn_cache)


def solution(mesh):
    return jax.shard_map(
        on_device,
        mesh=mesh,
        in_specs=(
            P(("seq", "head"), None),
            P(("seq", "head"), None),
            P(("seq", "head"), None),
            P(("seq", "head"), None),
            P("seq", "head"),
            P("head", None),
            P("head", "seq"),
            P(),
            P(),
        ),
        out_specs=(P(("seq", "head"), None), P("seq", "head")),
        check_vma=False,
    )
```

profile of v0, /device:TPU:1, one launch (start us, length us, event | category | flops | bytes accessed | tf_op | source)
XLA Modules:
  0.0 524.4 jit_solution(14958218900907158052)
XLA Ops:
  7.2 0.0 copy-start
  7.2 0.0 all-gather.4.cloned.1.call-start
  7.2 1.0 copy.47
  8.2 10.7 %all_to_all.54 = bf16[32,4,640]{2,0,1:T(8,128)(2,1)} all-to-all(bf16[32,4,640]{2,0,1:T(8,128)(2,1)S(1)} %bitcast.44), channel_id=1, replica_groups=mesh['seq'=64,'head'=4] {'head'}, dimensions={1} | all-to-all | bytes 327680 | tf_op jit(solution)/shard_map/all_to_all | solution.py:24
  18.9 0.0 all-gather.4.cloned.1.call-update
  18.9 0.0 all-gather.6.cloned.1.call-start
  19.0 0.9 copy.46
  19.9 8.0 %all_to_all.55 = bf16[32,4,640]{2,0,1:T(8,128)(2,1)} all-to-all(bf16[32,4,640]{2,0,1:T(8,128)(2,1)S(1)} %bitcast.45), channel_id=1, replica_groups=mesh['seq'=64,'head'=4] {'head'}, dimensions={1} | all-to-all | bytes 327680 | tf_op jit(solution)/shard_map/all_to_all | solution.py:25
  27.9 0.0 all-gather.6.cloned.1.call-update
  28.0 0.0 all-gather.8.cloned.1.call-start
  28.0 0.7 all-gather.8.cloned.1.call-update
  28.7 0.0 reduce-scatter.2.cloned.1.call-start
  28.8 0.9 copy.48
  29.7 8.7 %all_to_all.56 = bf16[32,4,640]{2,0,1:T(8,128)(2,1)S(1)} all-to-all(bf16[32,4,640]{2,0,1:T(8,128)(2,1)S(1)} %bitcast.46), channel_id=1, replica_groups=mesh['seq'=64,'head'=4] {'head'}, dimensions={1} | all-to-all | bytes 327680 | tf_op jit(solution)/shard_map/all_to_all | solution.py:23
  38.4 0.2 reshape.32
  38.6 145.0 %all-gather.4.cloned.1.call-done = bf16[8192,640]{1,0:T(8,128)(2,1)} async-done(((bf16[128,640]{1,0:T(8,128)(2,1)}), bf16[8192,640]{1,0:T(8,128)(2,1)}) %all-gather.4.cloned.1.call-update) | async-done | bytes 10485776 | tf_op jit(solution)/shard_map/all_gather | solution.py:33
  183.6 14.4 %copy.29 = bf16[8192,640]{0,1:T(8,128)(2,1)} copy(bf16[8192,640]{1,0:T(8,128)(2,1)} %all-gather.4.cloned.1.call-done) | data formatting | bytes 20971520 | tf_op jit(solution)/shard_map/all_gather | solution.py:33
  198.0 149.8 %all-gather.6.cloned.1.call-done = bf16[8192,640]{1,0:T(8,128)(2,1)} async-done(((bf16[128,640]{1,0:T(8,128)(2,1)}), bf16[8192,640]{1,0:T(8,128)(2,1)}) %all-gather.6.cloned.1.call-update) | async-done | bytes 10485776 | tf_op jit(solution)/shard_map/all_gather | solution.py:34
  347.8 14.4 %copy.33 = bf16[8192,640]{0,1:T(8,128)(2,1)} copy(bf16[8192,640]{1,0:T(8,128)(2,1)} %all-gather.6.cloned.1.call-done) | data formatting | bytes 20971520 | tf_op jit(solution)/shard_map/all_gather | solution.py:34
  362.2 13.8 %multiply_reduce_fusion = (f32[5,128]{1,0:T(8,128)S(1)}, f32[5,128,8192]{2,1,0:T(8,128)}) fusion(bf16[8192,5,128]{0,2,1:T(8,128)(2,1)} %bitcast.35, bf16[128,5,128]{2,1,0:T(8,128)(2,1)S(1)} %reshape.32), kind=kOutput, calls=%fused_computation.1 | convolution fusion | flops 1352662400 | bytes 31623680 | tf_op jit(solution)/shard_map/rhd,nhd->hrn/dot_general | solution.py:39
  376.0 9.6 %fusion = f32[5,128]{1,0:T(8,128)S(1)} fusion(f32[5,128,8192]{2,1,0:T(8,128)} %get-tuple-element.11, f32[5,128]{1,0:T(8,128)S(1)} %broadcast_maximum_fusion), kind=kLoop, calls=%fused_computation.2 | loop fusion | flops 15728000 | bytes 20976640 | tf_op jit(solution)/shard_map/reduce_sum | solution.py:44
  385.6 0.0 slice-start.1
  385.7 0.0 copy-start.2
  385.7 12.4 %fusion.14 = bf16[128,5,128]{0,2,1:T(8,128)(2,1)S(1)} fusion(bf16[8192,5,128]{0,2,1:T(8,128)(2,1)} %bitcast.38, f32[5,128,8192]{2,1,0:T(8,128)} %get-tuple-element.11, f32[5,128]{1,0:T(8,128)S(1)} %broadcast_maximum_fusion, f32[128,5]{0,1:T(8,128)S(1)} %bitcast.50), kind=kOutput, calls=%fused_computation.13 | convolution fusion | flops 1358069760 | bytes 31626240 | tf_op jit(solution)/shard_map/hrn,nhd->hrd/dot_general | solution.py:45
  398.1 0.0 copy-start.3
  398.1 1.2 convolution_multiply_fusion.1
  399.4 85.7 %all-gather.8.cloned.1.call-done = bf16[640,5120]{0,1:T(8,128)(2,1)} async-done(((bf16[640,80]{0,1:T(8,128)(2,1)}), bf16[640,5120]{0,1:T(8,128)(2,1)}) %all-gather.8.cloned.1.call-update) | async-done | bytes 6553616 | tf_op jit(solution)/shard_map/all_gather | solution.py:14
  485.1 6.1 %fusion.7 = bf16[128,5120]{1,0:T(8,128)(2,1)} fusion(f32[128,5120]{1,0:T(8,128)S(1)} %convolution_multiply_fusion.1, bf16[128,640]{1,0:T(8,128)(2,1)S(1)} %copy-done, bf16[640,5120]{0,1:T(8,128)(2,1)} %all-gather.8.cloned.1.call-done, f32[5120]{0:T(1024)S(1)} %copy-done.3), kind=kOutput, calls=%fused_computation.10 | convolution fusion | flops 840826880 | bytes 10670080 | tf_op jit(solution)/shard_map/dot_general | solution.py:12
  491.2 0.0 reduce-scatter.2.cloned.1.call-update
  491.3 0.8 copy.34
  492.1 24.0 %reduce-scatter.2.cloned.1.call-done = bf16[32,5120]{1,0:T(8,128)(2,1)} async-done(((bf16[128,5120]{1,0:T(8,128)(2,1)}), bf16[32,5120]{1,0:T(8,128)(2,1)}) %reduce-scatter.2.cloned.1.call-update) | async-done | bytes 327696 | tf_op jit(solution)/shard_map/reduce_scatter | solution.py:55
  516.1 1.8 add_convert_fusion
  (10 shorter events, 0.0 us)
Async XLA Ops:
  7.2 478.0 %copy-start = (bf16[128,640]{1,0:T(8,128)(2,1)S(1)}, bf16[128,640]{1,0:T(8,128)(2,1)}, u32[]{:S(2)}) copy-start(bf16[128,640]{1,0:T(8,128)(2,1)} %param.13) | copy-start | bytes 491524
  7.2 176.5 %all-gather.4.cloned.1.call-start = ((), (), s32[]{:S(2)}) async-start(), calls=%async_computation.4 | async-start | bytes 10649600 | tf_op jit(solution)/shard_map/all_gather | solution.py:33
  18.9 328.9 %all-gather.6.cloned.1.call-start = ((), (), s32[]{:S(2)}) async-start(), calls=%async_computation.5 | async-start | bytes 10649600 | tf_op jit(solution)/shard_map/all_gather | solution.py:34
  28.0 457.1 %all-gather.8.cloned.1.call-start = ((), (), s32[]{:S(2)}) async-start(), calls=%async_computation.6 | async-start | bytes 6656000 | tf_op jit(solution)/shard_map/all_gather | solution.py:14
  28.7 487.3 %reduce-scatter.2.cloned.1.call-start = ((), (), s32[]{:S(2)}) async-start(), calls=%async_computation.7 | async-start | bytes 1638400 | tf_op jit(solution)/shard_map/reduce_scatter | solution.py:55
  376.0 22.1 %slice-start = ((s8[6553600]{0:T(1024)(128)(4,1)}), s8[4194304]{0:T(1024)(128)(4,1)S(1)}, s32[]{:S(2)}) async-start(s8[6553600]{0:T(1024)(128)(4,1)} %bitcast.36), calls=%async_computation.8 | async-start | bytes 8388608
  385.6 12.5 %slice-start.1 = ((s8[6553600]{0:T(1024)(128)(4,1)}), s8[2359296]{0:T(1024)(128)(4,1)S(1)}, s32[]{:S(2)}) async-start(s8[6553600]{0:T(1024)(128)(4,1)} %bitcast.36), calls=%async_computation.9 | async-start | bytes 4718592
  385.7 12.5 %copy-start.2 = (f32[5120]{0:T(1024)S(1)}, f32[5120]{0:T(1024)}, u32[]{:S(2)}) copy-start(f32[5120]{0:T(1024)} %param.16) | copy-start | bytes 61444
  398.1 87.0 %copy-start.3 = (f32[5120]{0:T(1024)S(1)}, f32[5120]{0:T(1024)}, u32[]{:S(2)}) copy-start(f32[5120]{0:T(1024)} %param.17) | copy-start | bytes 61444
  399.4 116.7 %copy-start.1 = (bf16[32,5120]{1,0:T(8,128)(2,1)S(1)}, bf16[32,5120]{1,0:T(8,128)(2,1)}, u32[]{:S(2)}) copy-start(bf16[32,5120]{1,0:T(8,128)(2,1)} %param.12) | copy-start | bytes 983044
Sparse Core Ops, SparseCore 0:
  19.0 164.5 all-gather.3
  187.1 160.6 all-gather.5
  351.3 133.7 all-gather.7
  491.4 24.6 reduce-scatter.1
where the time goes:
time: 525 us; the launch traced here: 524 us
  waiting for transfers between devices  405 us (77%)
  matrix products  33.6 us (6%)
  local copies, waits for them, and re-layouts  32.6 us (6%)
  blocking collectives  27.5 us (5%)
  between operations  13.9 us (3%)
  other arithmetic  11.4 us (2%)
    all_gather x1, waiting for transfers between devices, on_device(): value_piece = lax.all_gather(value_part, 'seq', axis=0, tiled=True)  150 us
    all_gather x1, waiting for transfers between devices, on_device(): key_piece = lax.all_gather(key_part, 'seq', axis=0, tiled=True)  145 us
    all_gather x1, waiting for transfers between devices, column_product(): lax.all_gather(out_weight_b, 'seq', axis=1, tiled=True)  85.7 us
    reduce_scatter x1, waiting for transfers between devices, on_device(): lax.psum_scatter((gate_a * first_rows + gate_b * branch_b).astype(jnp.bfl...  24 us
    all_gather x1, local copies, waits for them, and re-layouts, on_device(): value_piece = lax.all_gather(value_part, 'seq', axis=0, tiled=True)  14.4 us
    all_gather x1, local copies, waits for them, and re-layouts, on_device(): key_piece = lax.all_gather(key_part, 'seq', axis=0, tiled=True)  14.4 us
    dot_general x1, matrix products, on_device(): jnp.einsum('rhd,nhd->hrn', query_heads, key_heads, preferred_element_type...  13.8 us
    dot_general x1, matrix products, on_device(): jnp.einsum('hrn,nhd->hrd', weights.astype(jnp.bfloat16), value_heads, pre...  12.4 us
  transfers between devices with their start and end apart: 4, of which 4 were waited for; matrix products, arithmetic and copies ran while one was open for 13% of the time, Pallas kernels for 0%

commit v1 on v0

v1 whole, which is shorter than its diff:
```python
import math
import jax
import jax.numpy as jnp
from jax import lax
from jax.experimental import pallas as pl
from jax.experimental.pallas import tpu as pltpu
from jax.sharding import PartitionSpec as P

MESH = pl.DeviceIdType.MESH
BF = jnp.bfloat16
F32 = jnp.float32
HD = 128
EXP2_SCALE = math.log2(math.e) / math.sqrt(HD)


def place():
    s, h = lax.axis_index("seq"), lax.axis_index("head")
    return (s // 4) % 2 * 2 + h // 2, s % 4, s // 8, h % 2


def device(x, y, z, c):
    return (z * 8 + x // 2 * 4 + y, x % 2 * 2 + c)


def send(src, dst, ssem, rsem, to):
    return pltpu.make_async_remote_copy(
        src_ref=src, dst_ref=dst, send_sem=ssem, recv_sem=rsem, device_id=to, device_id_type=MESH
    )


def attention_kernel(
    q_in, k_in, v_in, cache_out,
    q_pack, kv_pack, kvm_pack, q_buf, kv, kvm, m_ref, l_ref, ot, o_buf, st_buf, o_rcv, m_rcv, st_rcv, stm_rcv, c_res, m_res, attn,
    xs_sem, xr_sem, ys_sem, yr_sem, zs_sem, zr_sem, os_sem, or_sem, bs_sem, br_sem,
):
    x, y, z, c = place()
    me = x * 2 + c
    up, down = device(x, y, (z + 1) % 8, c), device(x, y, (z + 7) % 8, c)
    x_peer = [None] + [(me + d) % 8 for d in range(1, 8)]
    x_dev = [None] + [device(p // 2, y, z, p % 2) for p in x_peer[1:]]

    barrier = pltpu.get_barrier_semaphore()
    peers = x_dev[1:] + [up, down]
    for d in range(1, 4):
        for cc in range(2):
            peers.append(device(x, (y + d) % 4, z, cc))
    for p in peers:
        pl.semaphore_signal(barrier, inc=1, device_id=p, device_id_type=MESH)

    for p in range(8):
        xx, cc = p // 2, p % 2
        heads = (5 * xx + 3 * cc, 5 * xx + 3 * cc + 1, 5 * xx + 2)
        for i, hh in enumerate(heads):
            cols = slice(hh * HD, (hh + 1) * HD)
            q_pack[p, i] = q_in[:, cols]
            if i < 2:
                kv_pack[p, i, 0] = k_in[:, cols]
                kv_pack[p, i, 1] = v_in[:, cols]
            elif cc == 0:
                kvm_pack[xx, 0] = k_in[:, cols]
                kvm_pack[xx, 1] = v_in[:, cols]
    q_buf[0, :, me] = q_pack[me]
    kv[0, :, me] = kv_pack[me]
    kvm[0, x] = kvm_pack[x]
    pl.semaphore_wait(barrier, len(peers))

    xq, xa, xb, xm = [], [], [], []
    for d in range(1, 8):
        xq.append(send(q_pack.at[x_peer[d]], q_buf.at[0, :, me], xs_sem.at[0, d], xr_sem.at[0, d], x_dev[d]))
        xq[-1].start()
    for i, l in ((0, xa), (1, xb)):
        for d in range(1, 8):
            l.append(send(kv_pack.at[x_peer[d], i], kv.at[0, i, me], xs_sem.at[1 + i, d], xr_sem.at[1 + i, d], x_dev[d]))
            l[-1].start()
    for d in range(1, 4):
        xx = (x + d) % 4
        xm.append(send(kvm_pack.at[xx], kvm.at[0, x], xs_sem.at[3, d], xr_sem.at[3, d], device(xx, y, z, c)))
        xm[-1].start()

    for cp in xq:
        cp.wait_recv()
    yq = []
    for d in range(1, 4):
        yq.append(send(q_buf.at[0], q_buf.at[d], ys_sem.at[d], yr_sem.at[d], device(x, (y + d) % 4, z, c)))
        yq[-1].start()

    def part_ref(part, slot):
        return kvm.at[slot] if part == 2 else kv.at[slot, part]

    def ring(part, step, way):
        src = 0 if step == 1 else 2 * (step - 1) - 1 + way
        dst = 7 if step == 4 else 2 * step - 1 + way
        return send(part_ref(part, src), part_ref(part, dst), zs_sem.at[part, step, way], zr_sem.at[part, step, way], (up, down)[way])

    rings = []
    def start_ring(part, step):
        ways = (0, 1) if step < 4 else ((0,) if part == 0 else (1,))
        for way in ways:
            cp = ring(part, step, way)
            cp.start()
            rings.append(cp)

    def wait_ring(part, step):
        ways = (0, 1) if step < 4 else ((0,) if part == 0 else (1,))
        for way in ways:
            ring(part, step, way).wait_recv()

    for part, l in ((0, xa), (1, xb), (2, xm)):
        for cp in l:
            cp.wait_recv()
        start_ring(part, 1)

    def attend(lo, n, first):
        for head in range(3):
            def tile(t, _):
                if head < 2:
                    kk = kv[lo:lo + n, head, :, 0].reshape(n * 256, HD)
                    vv = kv[lo:lo + n, head, :, 1].reshape(n * 256, HD)
                else:
                    kk = kvm[lo:lo + n, :, 0].reshape(n * 128, HD)
                    vv = kvm[lo:lo + n, :, 1].reshape(n * 128, HD)
                qq = q_buf[t, head].reshape(256, HD)
                s = lax.dot_general(kk, qq, (((1,), (1,)), ((), ())), preferred_element_type=F32)
                top = jnp.max(s, axis=0, keepdims=True)
                if not first:
                    old = m_ref[head, t]
                    top = jnp.maximum(top, old)
                    fade = jnp.exp2((old - top) * EXP2_SCALE)
                p = jnp.exp2(s * EXP2_SCALE - top * EXP2_SCALE)
                tot = jnp.sum(p, axis=0, keepdims=True)
                o = lax.dot_general(vv, p.astype(BF), (((0,), (0,)), ((), ())), preferred_element_type=F32)
                if first:
                    l_ref[head, t] = tot
                    ot[head, t] = o
                else:
                    l_ref[head, t] = l_ref[head, t] * fade + tot
                    ot[head, t] = ot[head, t] * fade + o
                m_ref[head, t] = top
                return 0
            lax.fori_loop(0, 4, tile, 0)

    for cp in yq:
        cp.wait_recv()
    attend(0, 1, True)
    for step in range(1, 5):
        for part in range(3):
            wait_ring(part, step)
            if step < 4:
                if step < 3 or True:
                    pass
                start_ring(part, step + 1)
        if step < 4:
            attend(2 * step - 1, 2, False)
    attend(7, 1, False)

    outs = []
    m_slot = c
    for t in (1, 2, 3, 0):
        for head in range(3):
            l = l_ref[head, t]
            o = (ot[head, t] / l).astype(BF)
            lse = m_ref[head, t] * EXP2_SCALE + jnp.log2(l)
            for half in range(2):
                cols = slice(half * HD, (half + 1) * HD)
                o_buf[t, half, head] = o[:, cols]
                st_buf[t, half, head:head + 1] = lse[:, cols]
        yy = (y + 4 - t) % 4
        same, other = device(x, yy, z, c), device(x, yy, z, 1 - c)
        if t > 0:
            outs.append(send(o_buf.at[t, :, 0:2], o_rcv.at[t], os_sem.at[t, 0], or_sem.at[t, 0], same))
            outs.append(send(st_buf.at[t], st_rcv.at[t], os_sem.at[t, 1], or_sem.at[t, 1], same))
            outs.append(send(o_buf.at[t, c, 2], m_rcv.at[t, 0], os_sem.at[t, 2], or_sem.at[t, 2], same))
        outs.append(send(o_buf.at[t, 1 - c, 2], m_rcv.at[t, 1], os_sem.at[t, 3], or_sem.at[t, 3], other))
        outs.append(send(st_buf.at[t, 1 - c], stm_rcv.at[t], os_sem.at[t, 4], or_sem.at[t, 4], other))
        for cp in outs[-(5 if t > 0 else 2):]:
            cp.start()
    for cp in outs:
        cp.wait_recv()

    def merge(parts):
        top = parts[0][1]
        for _, s in parts[1:]:
            top = jnp.maximum(top, s)
        acc, tot = 0.0, 0.0
        for o, s in parts:
            w = jnp.exp2(s - top)
            acc = acc + o.astype(F32) * w
            tot = tot + w
        return (acc / tot).T.astype(BF)

    for half in range(2):
        for head in range(2):
            parts = [(o_buf[0, half, head], st_buf[0, half, head:head + 1])]
            for d in range(1, 4):
                parts.append((o_rcv[d, half, head], st_rcv[d, half, head:head + 1]))
            c_res[half, head] = merge(parts)
    parts = [(o_buf[0, c, 2], st_buf[0, c, 2:3])]
    for d in range(4):
        if d > 0:
            parts.append((m_rcv[d, 0], st_rcv[d, c, 2:3]))
        parts.append((m_rcv[d, 1], stm_rcv[d, 2:3]))
    m_res[...] = merge(parts)

    def back(half):
        to_x, to_c = 2 * half + x // 2, x % 2
        own = (to_x == x) & (to_c == c)
        return own, device(to_x, y, z, to_c)

    ab = []
    for half in range(2):
        own, to = back(half)
        cp = send(c_res.at[half], attn.at[pl.ds(3 * c, 2)], bs_sem.at[half], br_sem.at[c], to)
        loc = pltpu.make_async_copy(c_res.at[half], attn.at[pl.ds(3 * c, 2)], br_sem.at[c])
        ab.append((own, cp))
        @pl.when(own)
        def _():
            loc.start()
        @pl.when(jnp.logical_not(own))
        def _():
            cp.start()
    to_x, to_c = 2 * c + x // 2, x % 2
    m_own = (to_x == x) & (to_c == c)
    mcp = send(m_res, attn.at[2], bs_sem.at[2], br_sem.at[2], device(to_x, y, z, to_c))
    mloc = pltpu.make_async_copy(m_res, attn.at[2], br_sem.at[2])
    @pl.when(m_own)
    def _():
        mloc.start()
    @pl.when(jnp.logical_not(m_own))
    def _():
        mcp.start()
    pltpu.make_async_copy(c_res.at[0], attn.at[0:2], br_sem.at[0]).wait()
    pltpu.make_async_copy(c_res.at[0], attn.at[3:5], br_sem.at[1]).wait()
    pltpu.make_async_copy(m_res, attn.at[2], br_sem.at[2]).wait()
    for i in range(5):
        cache_out[:, i * HD:(i + 1) * HD] = attn[i]

    for cp in xq + xa + xb + xm + yq + rings + outs:
        cp.wait_send()
    for own, cp in ab + [(m_own, mcp)]:
        @pl.when(jnp.logical_not(own))
        def _():
            cp.wait_send()


def attention(q, k, v):
    vm = pl.BlockSpec(memory_space=pltpu.VMEM)
    D = pltpu.SemaphoreType.DMA
    V = pltpu.VMEM
    return pl.pallas_call(
        attention_kernel,
        out_shape=jax.ShapeDtypeStruct((128, 640), BF),
        in_specs=[vm] * 3,
        out_specs=vm,
        scratch_shapes=[
            V((8, 3, 32, HD), BF), V((8, 2, 2, 32, HD), BF), V((4, 2, 32, HD), BF),
            V((4, 3, 8, 32, HD), BF),
            V((8, 2, 8, 2, 32, HD), BF), V((8, 4, 2, 32, HD), BF),
            V((3, 4, 1, 256), F32), V((3, 4, 1, 256), F32), V((3, 4, HD, 256), F32),
            V((4, 2, 3, HD, HD), BF), V((4, 2, 8, HD), F32),
            V((4, 2, 2, HD, HD), BF), V((4, 2, HD, HD), BF), V((4, 2, 8, HD), F32), V((4, 8, HD), F32),
            V((2, 2, HD, HD), BF), V((HD, HD), BF), V((5, HD, HD), BF),
            D((4, 8)), D((4, 8)), D((4,)), D((4,)), D((3, 5, 2)), D((3, 5, 2)), D((4, 5)), D((4, 5)), D((3,)), D((3,)),
        ],
        compiler_params=pltpu.CompilerParams(collective_id=1, has_side_effects=True, vmem_limit_bytes=48 * 2**20),
        name="attention",
    )(q, k, v)


def on_device(
    queries, keys, values, residual, cached_context, out_weight_a, out_weight_b, gate_a, gate_b
):
    attn_cache = attention(queries, keys, values)
    branch_b = jnp.dot(
        cached_context,
        lax.all_gather(out_weight_b, "seq", axis=1, tiled=True),
        preferred_element_type=F32,
    )
    first_rows = jnp.dot(attn_cache, out_weight_a, preferred_element_type=F32)
    summed = lax.psum_scatter(
        (gate_a * first_rows + gate_b * branch_b).astype(BF), "head", scatter_dimension=0, tiled=True
    ).astype(F32)
    mixed = (residual.astype(F32) + summed).astype(BF)
    return (mixed, attn_cache)


def solution(mesh):
    tokens = P(("seq", "head"), None)
    return jax.shard_map(
        on_device,
        mesh=mesh,
        in_specs=(tokens, tokens, tokens, tokens, P("seq", "head"), P("head", None), P("head", "seq"), P(), P()),
        out_specs=(tokens, P("seq", "head")),
        check_vma=False,
    )
```

time: 525 us -> 194 us (0.37)
  waiting for transfers between devices: 405 us -> 86.6 us
  Pallas kernels: 0 us -> 77.5 us
  local copies, waits for them, and re-layouts: 32.6 us -> 3.43 us
  blocking collectives: 27.5 us -> 0 us
  matrix products: 33.6 us -> 10.2 us
  other arithmetic: 11.4 us -> 1.77 us
    all_gather x3 -> x1, waiting for transfers between devices: 381 us -> 61.1 us  [on_device(): lax.all_gather(out_weight_b, 'seq', axis=1, tiled=True)]
    pallas_call x0 -> x1, Pallas kernels: none -> 77.5 us  [attention(): pl.pallas_call(attention_kernel, out_shape=jax.ShapeDtypeStruct((128, 640...]
    all_gather x2 -> x0, local copies, waits for them, and re-layouts: 28.7 us -> none  [the longest x1 14.4 us: on_device(): value_piece = lax.all_gather(value_part, 'seq', axis=0, tiled=True)]
    all_to_all x3 -> x0, blocking collectives: 27.5 us -> none  [the longest x1 10.7 us: on_device(): lax.all_to_all(keys, 'head', split_axis=1, concat_axis=0, tiled=True)]
    dot_general x4 -> x2, matrix products: 33.6 us -> 10.2 us  [the longest x1 6.08 us: on_device(): jnp.dot(cached_context, lax.all_gather(out_weight_b, 'seq', axis=1, tiled...]
    reduce_sum x1 -> x0, other arithmetic: 9.61 us -> none  [on_device(): new_sum = jnp.sum(weights, axis=2)]
  transfers between devices with their start and end apart: 4 -> 2, of which waited for: 4 -> 2; matrix products, arithmetic and copies ran while one was open for 13% -> 2% of each run, Pallas kernels for 0% -> 40%
where the time goes in v1:
time: 194 us
  waiting for transfers between devices  86.6 us (45%)
  Pallas kernels  77.5 us (40%)
  between operations  14.1 us (7%)
  matrix products  10.2 us (5%)
  local copies, waits for them, and re-layouts  3.43 us (2%)
    pallas_call x1, Pallas kernels, attention(): pl.pallas_call(attention_kernel, out_shape=jax.ShapeDtypeStruct((128, 640...  77.5 us
    all_gather x1, waiting for transfers between devices, on_device(): lax.all_gather(out_weight_b, 'seq', axis=1, tiled=True)  61.1 us
    reduce_scatter x1, waiting for transfers between devices, on_device(): lax.psum_scatter((gate_a * first_rows + gate_b * branch_b).astype(BF), 'h...  24.8 us
    dot_general x1, matrix products, on_device(): jnp.dot(cached_context, lax.all_gather(out_weight_b, 'seq', axis=1, tiled...  6.08 us
    dot_general x1, matrix products, on_device(): first_rows = jnp.dot(attn_cache, out_weight_a, preferred_element_type=F32)  4.09 us
  transfers between devices with their start and end apart: 2, of which 2 were waited for; matrix products, arithmetic and copies ran while one was open for 2% of the time, Pallas kernels for 40%

profile of v1, /device:TPU:1, one launch (start us, length us, event | category | flops | bytes accessed | tf_op | source)
XLA Modules:
  0.0 193.6 jit_solution(4224114791554937470)
XLA Ops:
  7.2 0.0 copy-start
  7.2 0.0 all-gather.2.cloned.1.call-start
  7.2 0.7 all-gather.2.cloned.1.call-update
  7.9 0.0 reduce-scatter.2.cloned.1.call-start
  8.0 0.0 copy-start.1
  8.0 0.9 copy-done.1
  8.9 0.0 copy-start.2
  8.9 0.9 copy-done.2
  9.8 0.0 copy-start.3
  9.8 0.9 copy-done.3
  10.7 77.5 %attention.1 = bf16[128,640]{1,0:T(8,128)(2,1)S(1)} custom-call(bf16[32,2560]{1,0:T(8,128)(2,1)S(1)} %copy-done.1, bf16[32,2560]{1,0:T(8,128)(2,1)S(1)} %copy-done.2, bf16[32,2560]{1,0:T(8,128)(2,1)S(1)} %copy-done.3), custom_call_target="tpu_custom_call" | custom-call | tf_op jit(solution)/shard_map/attention/pallas_call | solution.py:249
  88.2 0.0 copy-start.5
  88.2 4.1 %convolution_multiply_fusion.1 = f32[128,5120]{1,0:T(8,128)S(1)} fusion(bf16[128,640]{1,0:T(8,128)(2,1)S(1)} %attention.1, bf16[640,5120]{1,0:T(8,128)(2,1)} %param.14, f32[5120]{0:T(1024)} %param.16), kind=kOutput, calls=%fused_computation.2 | convolution fusion | flops 839516160 | bytes 9359360 | tf_op jit(solution)/shard_map/dot_general | solution.py:278
  92.3 0.0 copy-start.4
  92.3 61.1 %all-gather.2.cloned.1.call-done = bf16[640,5120]{0,1:T(8,128)(2,1)} async-done(((bf16[640,80]{0,1:T(8,128)(2,1)}), bf16[640,5120]{0,1:T(8,128)(2,1)}) %all-gather.2.cloned.1.call-update) | async-done | bytes 6553616 | tf_op jit(solution)/shard_map/all_gather | solution.py:275
  153.4 0.0 copy-done
  153.4 0.0 copy-done.5
  153.4 6.1 %fusion.1 = bf16[128,5120]{1,0:T(8,128)(2,1)} fusion(f32[128,5120]{1,0:T(8,128)S(1)} %convolution_multiply_fusion.1, bf16[128,640]{1,0:T(8,128)(2,1)S(1)} %copy-done, bf16[640,5120]{0,1:T(8,128)(2,1)} %all-gather.2.cloned.1.call-done, f32[5120]{0:T(1024)S(1)} %copy-done.5), kind=kOutput, calls=%fused_computation.3 | convolution fusion | flops 840826880 | bytes 10670080 | tf_op jit(solution)/shard_map/dot_general | solution.py:273
  159.4 0.0 reduce-scatter.2.cloned.1.call-update
  159.5 24.8 %reduce-scatter.2.cloned.1.call-done = bf16[32,5120]{1,0:T(8,128)(2,1)} async-done(((bf16[128,5120]{1,0:T(8,128)(2,1)}), bf16[32,5120]{1,0:T(8,128)(2,1)}) %reduce-scatter.2.cloned.1.call-update) | async-done | bytes 327696 | tf_op jit(solution)/shard_map/reduce_scatter | solution.py:279
  184.3 0.0 copy-done.4
  184.3 1.8 add_convert_fusion
  186.1 0.7 copy.12
Async XLA Ops:
  7.2 146.2 %copy-start = (bf16[128,640]{1,0:T(8,128)(2,1)S(1)}, bf16[128,640]{1,0:T(8,128)(2,1)}, u32[]{:S(2)}) copy-start(bf16[128,640]{1,0:T(8,128)(2,1)} %param.13) | copy-start | bytes 491524
  7.2 146.2 %all-gather.2.cloned.1.call-start = ((), (), s32[]{:S(2)}) async-start(), calls=%async_computation.1 | async-start | bytes 6656000 | tf_op jit(solution)/shard_map/all_gather | solution.py:275
  7.9 176.4 %reduce-scatter.2.cloned.1.call-start = ((), (), s32[]{:S(2)}) async-start(), calls=%async_computation.2 | async-start | bytes 1638400 | tf_op jit(solution)/shard_map/reduce_scatter | solution.py:279
  8.0 0.9 copy-start.1
  8.9 0.9 copy-start.2
  9.8 0.9 copy-start.3
  88.2 65.2 %copy-start.5 = (f32[5120]{0:T(1024)S(1)}, f32[5120]{0:T(1024)}, u32[]{:S(2)}) copy-start(f32[5120]{0:T(1024)} %param.17) | copy-start | bytes 61444
  92.3 92.0 %copy-start.4 = (bf16[32,5120]{1,0:T(8,128)(2,1)S(1)}, bf16[32,5120]{1,0:T(8,128)(2,1)}, u32[]{:S(2)}) copy-start(bf16[32,5120]{1,0:T(8,128)(2,1)} %param.12) | copy-start | bytes 983044
Sparse Core Ops, SparseCore 0:
  11.5 141.8 all-gather.1
  159.6 24.6 reduce-scatter.1

commit v2 on v1

--- a/solution.py
+++ b/solution.py
@@ -28,10 +28,14 @@
     )
 
 
-def attention_kernel(
-    q_in, k_in, v_in, cache_out,
+def window_kernel(
+    q_hbm, k_hbm, v_hbm, res_hbm, ctx_hbm, wa_hbm, wb_hbm, ga_hbm, gb_hbm, mixed_out, cache_out,
+    q_in, k_in, v_in, res, wa, wb, ga, gb,
     q_pack, kv_pack, kvm_pack, q_buf, kv, kvm, m_ref, l_ref, ot, o_buf, st_buf, o_rcv, m_rcv, st_rcv, stm_rcv, c_res, m_res, attn,
-    xs_sem, xr_sem, ys_sem, yr_sem, zs_sem, zr_sem, os_sem, or_sem, bs_sem, br_sem,
+    w_all, ctx, b_part, b_rcv1, b_snd2, b_keep, b_rcv2, b_snd3, b_rcv3, base,
+    a_rows, p_snd1, p_keep1, p_rcv1, p_snd2, p_rcv2,
+    in_sem, xs_sem, xr_sem, ys_sem, yr_sem, zs_sem, zr_sem, os_sem, or_sem, bs_sem, br_sem,
+    ws_sem, wr_sem, cs_sem, cr_sem, ds_sem, dr_sem, ps_sem, pr_sem,
 ):
     x, y, z, c = place()
     me = x * 2 + c
@@ -39,14 +43,29 @@
     x_peer = [None] + [(me + d) % 8 for d in range(1, 8)]
     x_dev = [None] + [device(p // 2, y, z, p % 2) for p in x_peer[1:]]
 
+    xl, xh = x % 2, x // 2
+    core_dev, pair_dev = device(x, y, z, 1 - c), device(xh * 2 + 1 - xl, y, z, c)
+    far_x = (1 - xh) * 2 + xl
+    loads = []
+    for i, (src, dst) in enumerate((
+        (q_hbm, q_in), (k_hbm, k_in), (v_hbm, v_in), (wb_hbm, wb), (ctx_hbm, ctx.at[0, 0]),
+        (gb_hbm, gb), (res_hbm, res), (ga_hbm, ga), (wa_hbm, wa),
+    )):
+        loads.append(pltpu.make_async_copy(src, dst, in_sem.at[i]))
+        loads[-1].start()
+
     barrier = pltpu.get_barrier_semaphore()
     peers = x_dev[1:] + [up, down]
     for d in range(1, 4):
         for cc in range(2):
             peers.append(device(x, (y + d) % 4, z, cc))
+        peers.append(device(far_x, (y + d) % 4, z, c))
     for p in peers:
         pl.semaphore_signal(barrier, inc=1, device_id=p, device_id_type=MESH)
 
+    for cp in loads[0:4]:
+        cp.wait()
+    w_all[z] = wb[...].T
     for p in range(8):
         xx, cc = p // 2, p % 2
         heads = (5 * xx + 3 * cc, 5 * xx + 3 * cc + 1, 5 * xx + 2)
@@ -77,12 +96,37 @@
         xm.append(send(kvm_pack.at[xx], kvm.at[0, x], xs_sem.at[3, d], xr_sem.at[3, d], device(xx, y, z, c)))
         xm[-1].start()
 
+    def w_ring(step, way):
+        at = (z + 9 - step) % 8 if way == 0 else (z + 7 + step) % 8
+        ref = w_all.at[at]
+        if step == 4:
+            ref = ref.at[0:48] if way == 0 else ref.at[48:80]
+        return send(ref, ref, ws_sem.at[step, way], wr_sem.at[step, way], (up, down)[way])
+
+    def w_start(step):
+        for way in range(2):
+            w_ring(step, way).start()
+
+    def w_wait(step):
+        for way in range(2):
+            cp = w_ring(step, way)
+            cp.wait_recv()
+            cp.wait_send()
+
+    w_start(1)
+
     for cp in xq:
         cp.wait_recv()
     yq = []
     for d in range(1, 4):
         yq.append(send(q_buf.at[0], q_buf.at[d], ys_sem.at[d], yr_sem.at[d], device(x, (y + d) % 4, z, c)))
         yq[-1].start()
+
+    loads[4].wait()
+    ctx_x = send(ctx.at[0, 0], ctx.at[0, 1], cs_sem.at[0], cr_sem.at[0], device(far_x, y, z, c))
+    ctx_x.start()
+    w_wait(1)
+    w_start(2)
 
     def part_ref(part, slot):
         return kvm.at[slot] if part == 2 else kv.at[slot, part]
@@ -139,18 +183,40 @@
                 return 0
             lax.fori_loop(0, 4, tile, 0)
 
+    w_wait(2)
+    w_start(3)
     for cp in yq:
         cp.wait_recv()
+    ctx_x.wait_recv()
+    ctx_y = []
+    for d in range(1, 4):
+        ctx_y.append(send(ctx.at[0], ctx.at[d], cs_sem.at[d], cr_sem.at[d], device(x, (y + d) % 4, z, c)))
+        ctx_y[-1].start()
+    w_wait(3)
+    w_start(4)
     attend(0, 1, True)
     for step in range(1, 5):
         for part in range(3):
             wait_ring(part, step)
             if step < 4:
-                if step < 3 or True:
-                    pass
                 start_ring(part, step + 1)
         if step < 4:
             attend(2 * step - 1, 2, False)
+        if step == 3:
+            w_wait(4)
+            for cp in ctx_y:
+                cp.wait_recv()
+
+            def b_tile(d, _):
+                part = lax.dot_general(
+                    ctx[d].reshape(256, 640), w_all[...].reshape(640, 640),
+                    (((1,), (1,)), ((), ())), preferred_element_type=F32,
+                )
+                b_part[d] = part.astype(BF).reshape(2, 2, 2, 32, 640)
+                return 0
+            lax.fori_loop(0, 4, b_tile, 0)
+            b_core = send(b_part.at[:, :, :, 1 - c], b_rcv1, ds_sem.at[0], dr_sem.at[0], core_dev)
+            b_core.start()
     attend(7, 1, False)
 
     outs = []
@@ -174,6 +240,17 @@
         outs.append(send(st_buf.at[t, 1 - c], stm_rcv.at[t], os_sem.at[t, 4], or_sem.at[t, 4], other))
         for cp in outs[-(5 if t > 0 else 2):]:
             cp.start()
+    b_core.wait_recv()
+
+    def b_sum1(d, _):
+        for e in range(2):
+            b_snd2[d, e] = (b_part[d, e, 1 - xl, c].astype(F32) + b_rcv1[d, e, 1 - xl].astype(F32)).astype(BF)
+            b_keep[d, e] = b_part[d, e, xl, c].astype(F32) + b_rcv1[d, e, xl].astype(F32)
+        return 0
+    lax.fori_loop(0, 4, b_sum1, 0)
+    b_pair = send(b_snd2, b_rcv2, ds_sem.at[1], dr_sem.at[1], pair_dev)
+    b_pair.start()
+
     for cp in outs:
         cp.wait_recv()
 
@@ -228,13 +305,61 @@
     @pl.when(jnp.logical_not(m_own))
     def _():
         mcp.start()
+    b_pair.wait_recv()
+
+    def b_sum2(d, _):
+        for e in range(2):
+            b_snd3[d, e] = (b_keep[d, e] + b_rcv2[d, e].astype(F32)).astype(BF)
+        return 0
+    lax.fori_loop(0, 4, b_sum2, 0)
+    q_me = xh * 4 + y
+    b_out = []
+    for d in range(4):
+        for e in range(2):
+            if d + e > 0:
+                to = device(far_x if e else x, (y + 4 - d) % 4, z, c)
+                b_out.append(send(b_snd3.at[d, e], b_rcv3.at[q_me], ds_sem.at[2 + 2 * d + e], dr_sem.at[2 + 2 * d + e], to))
+                b_out[-1].start()
+    b_rcv3[q_me] = b_snd3[0, 0]
     pltpu.make_async_copy(c_res.at[0], attn.at[0:2], br_sem.at[0]).wait()
     pltpu.make_async_copy(c_res.at[0], attn.at[3:5], br_sem.at[1]).wait()
     pltpu.make_async_copy(m_res, attn.at[2], br_sem.at[2]).wait()
     for i in range(5):
         cache_out[:, i * HD:(i + 1) * HD] = attn[i]
 
-    for cp in xq + xa + xb + xm + yq + rings + outs:
+    for i, (pl_x, pl_c) in enumerate(((1 - xl, 1 - c), (xl, 1 - c), (1 - xl, c), (xl, c))):
+        for head in range(5):
+            a_rows[i * 32:(i + 1) * 32, head * HD:(head + 1) * HD] = attn[head, pl.ds((pl_x * 2 + pl_c) * 32, 32)]
+    loads[8].wait()
+    stage1, stage2 = [], []
+    for j in range(5):
+        cols = slice(j * 1024, (j + 1) * 1024)
+        part = jnp.dot(a_rows[...], wa[:, cols], preferred_element_type=F32)
+        p_snd1[j] = part[0:64].astype(BF)
+        stage1.append(send(p_snd1.at[j], p_rcv1.at[j], ps_sem.at[0, j], pr_sem.at[0, j], core_dev))
+        stage1[-1].start()
+        p_keep1[j] = part[64:128]
+    for j in range(5):
+        stage1[j].wait_recv()
+        p_snd2[j] = (p_keep1[j, 0:32] + p_rcv1[j, 0:32].astype(F32)).astype(BF)
+        stage2.append(send(p_snd2.at[j], p_rcv2.at[j], ps_sem.at[1, j], pr_sem.at[1, j], pair_dev))
+        stage2[-1].start()
+
+    for cp in b_out:
+        cp.wait_recv()
+    for cp in loads[5:8]:
+        cp.wait()
+    for zz in range(8):
+        cols = slice(zz * 640, (zz + 1) * 640)
+        piece = jnp.concatenate([b_rcv3[qq, :, zz * 80:(zz + 1) * 80].astype(F32) for qq in range(8)], axis=1)
+        base[:, cols] = res[:, cols].astype(F32) + gb[:, cols] * piece
+    for j in range(5):
+        cols = slice(j * 1024, (j + 1) * 1024)
+        stage2[j].wait_recv()
+        total = p_keep1[j, 32:64] + p_rcv1[j, 32:64].astype(F32) + p_rcv2[j].astype(F32)
+        mixed_out[:, cols] = (base[:, cols] + ga[:, cols] * total).astype(BF)
+
+    for cp in xq + xa + xb + xm + yq + rings + outs + [ctx_x, b_core, b_pair] + ctx_y + b_out + stage1 + stage2:
         cp.wait_send()
     for own, cp in ab + [(m_own, mcp)]:
         @pl.when(jnp.logical_not(own))
@@ -242,16 +367,19 @@
             cp.wait_send()
 
 
-def attention(q, k, v):
+def window(q, k, v, res, ctx, wa, wb, ga, gb):
+    any_space = pl.BlockSpec(memory_space=pl.ANY)
     vm = pl.BlockSpec(memory_space=pltpu.VMEM)
     D = pltpu.SemaphoreType.DMA
     V = pltpu.VMEM
     return pl.pallas_call(
-        attention_kernel,
-        out_shape=jax.ShapeDtypeStruct((128, 640), BF),
-        in_specs=[vm] * 3,
-        out_specs=vm,
+        window_kernel,
+        out_shape=(jax.ShapeDtypeStruct((32, 5120), BF), jax.ShapeDtypeStruct((128, 640), BF)),
+        in_specs=[any_space] * 9,
+        out_specs=(vm, vm),
         scratch_shapes=[
+            V((32, 2560), BF), V((32, 2560), BF), V((32, 2560), BF), V((32, 5120), BF),
+            V((640, 5120), BF), V((640, 80), BF), V((1, 5120), F32), V((1, 5120), F32),
             V((8, 3, 32, HD), BF), V((8, 2, 2, 32, HD), BF), V((4, 2, 32, HD), BF),
             V((4, 3, 8, 32, HD), BF),
             V((8, 2, 8, 2, 32, HD), BF), V((8, 4, 2, 32, HD), BF),
@@ -259,34 +387,23 @@
             V((4, 2, 3, HD, HD), BF), V((4, 2, 8, HD), F32),
             V((4, 2, 2, HD, HD), BF), V((4, 2, HD, HD), BF), V((4, 2, 8, HD), F32), V((4, 8, HD), F32),
             V((2, 2, HD, HD), BF), V((HD, HD), BF), V((5, HD, HD), BF),
-            D((4, 8)), D((4, 8)), D((4,)), D((4,)), D((3, 5, 2)), D((3, 5, 2)), D((4, 5)), D((4, 5)), D((3,)), D((3,)),
+            V((8, 80, 640), BF), V((4, 2, HD, 640), BF), V((4, 2, 2, 2, 32, 640), BF), V((4, 2, 2, 32, 640), BF),
+            V((4, 2, 32, 640), BF), V((4, 2, 32, 640), F32), V((4, 2, 32, 640), BF), V((4, 2, 32, 640), BF),
+            V((8, 32, 640), BF), V((32, 5120), F32),
+            V((HD, 640), BF), V((5, 64, 1024), BF), V((5, 64, 1024), F32), V((5, 64, 1024), BF),
+            V((5, 32, 1024), BF), V((5, 32, 1024), BF),
+            D((9,)), D((4, 8)), D((4, 8)), D((4,)), D((4,)), D((3, 5, 2)), D((3, 5, 2)), D((4, 5)), D((4, 5)),
+            D((3,)), D((3,)), D((5, 2)), D((5, 2)), D((4,)), D((4,)), D((10,)), D((10,)), D((2, 5)), D((2, 5)),
         ],
-        compiler_params=pltpu.CompilerParams(collective_id=1, has_side_effects=True, vmem_limit_bytes=48 * 2**20),
-        name="attention",
-    )(q, k, v)
-
-
-def on_device(
-    queries, keys, values, residual, cached_context, out_weight_a, out_weight_b, gate_a, gate_b
-):
-    attn_cache = attention(queries, keys, values)
-    branch_b = jnp.dot(
-        cached_context,
-        lax.all_gather(out_weight_b, "seq", axis=1, tiled=True),
-        preferred_element_type=F32,
-    )
-    first_rows = jnp.dot(attn_cache, out_weight_a, preferred_element_type=F32)
-    summed = lax.psum_scatter(
-        (gate_a * first_rows + gate_b * branch_b).astype(BF), "head", scatter_dimension=0, tiled=True
-    ).astype(F32)
-    mixed = (residual.astype(F32) + summed).astype(BF)
-    return (mixed, attn_cache)
+        compiler_params=pltpu.CompilerParams(collective_id=1, has_side_effects=True, vmem_limit_bytes=56 * 2**20),
+        name="window",
+    )(q, k, v, res, ctx, wa, wb, ga.reshape(1, 5120), gb.reshape(1, 5120))
 
 
 def solution(mesh):
     tokens = P(("seq", "head"), None)
     return jax.shard_map(
-        on_device,
+        window,
         mesh=mesh,
         in_specs=(tokens, tokens, tokens, tokens, P("seq", "head"), P("head", None), P("head", "seq"), P(), P()),
         out_specs=(tokens, P("seq", "head")),

time: 194 us -> 103 us (0.53)
  waiting for transfers between devices: 86.6 us -> 0 us
  Pallas kernels: 77.5 us -> 97.1 us
  between operations: 14.1 us -> 0.64 us
  matrix products: 10.2 us -> 0 us
    all_gather x1 -> x0, waiting for transfers between devices: 61.1 us -> none  [on_device(): lax.all_gather(out_weight_b, 'seq', axis=1, tiled=True)]
    reduce_scatter x1 -> x0, waiting for transfers between devices: 24.8 us -> none  [on_device(): lax.psum_scatter((gate_a * first_rows + gate_b * branch_b).astype(BF), 'h...]
    pallas_call x1, Pallas kernels: 77.5 us -> 97.1 us  [window(): pl.pallas_call(window_kernel, out_shape=(jax.ShapeDtypeStruct((32, 5120),...]
    dot_general x2 -> x0, matrix products: 10.2 us -> none  [the longest x1 6.08 us: on_device(): jnp.dot(cached_context, lax.all_gather(out_weight_b, 'seq', axis=1, tiled...]
    unnamed x13 -> x3, local copies, waits for them, and re-layouts: 3.43 us -> 5.01 us
  transfers between devices with their start and end apart: 2 -> 0, of which waited for: 2 -> 0; matrix products, arithmetic and copies ran while one was open for 2% -> 0% of each run, Pallas kernels for 40% -> 0%
where the time goes in v2:
time: 103 us
  Pallas kernels  97.1 us (94%)
  local copies, waits for them, and re-layouts  5.01 us (5%)
    pallas_call x1, Pallas kernels, window(): pl.pallas_call(window_kernel, out_shape=(jax.ShapeDtypeStruct((32, 5120),...  97.1 us
    unnamed x3, local copies, waits for them, and re-layouts  5.01 us

profile of v2, /device:TPU:1, one launch (start us, length us, event | category | flops | bytes accessed | tf_op | source)
XLA Modules:
  0.0 102.7 jit_solution(3014260944416252595)
XLA Ops:
  0.6 1.7 %copy.11.wb_hbm = bf16[640,80]{1,0:T(8,128)(2,1)} copy(bf16[640,80]{0,1:T(8,128)(2,1)} %param.15) | data formatting | bytes 204800 | tf_op args[6]
  2.3 97.1 %window.1 = (bf16[32,5120]{1,0:T(8,128)(2,1)}, bf16[128,640]{1,0:T(8,128)(2,1)}) custom-call(bf16[32,2560]{1,0:T(8,128)(2,1)} %q_hbm.1, bf16[32,2560]{1,0:T(8,128)(2,1)} %k_hbm.1, bf16[32,2560]{1,0:T(8,128)(2,1)} %v_hbm.1, bf16[32,5120]{1,0:T(8,128)(2,1)} %res_hbm.1, bf16[128,640]{1,0:T(8,128)(2,1)} %ctx_hbm.1, bf16[640,5120]{1,0:T(8,128)(2,1)} %wa_hbm.1, ...), custom_call_target="tpu_custom_call" | custom-call | tf_op jit(solution)/shard_map/window/pallas_call | solution.py:375
  99.4 1.7 %copy.14 = bf16[32,5120]{1,0:T(8,128)(2,1)} copy(bf16[32,5120]{1,0:T(8,128)(2,1)} %get-tuple-element.4) | data formatting | bytes 655360
  101.1 1.6 %copy.15 = bf16[128,640]{1,0:T(8,128)(2,1)} copy(bf16[128,640]{1,0:T(8,128)(2,1)} %get-tuple-element.5) | data formatting | bytes 327680

commit v3 on v2

v3 whole, which is shorter than its diff:
```python
import math

import jax
import jax.numpy as jnp
from jax import lax
from jax.experimental import pallas as pl
from jax.experimental.pallas import tpu as pltpu
from jax.sharding import PartitionSpec as P

MESH = pl.DeviceIdType.MESH
BF = jnp.bfloat16
F32 = jnp.float32
HD = 128
EXP2_SCALE = math.log2(math.e) / math.sqrt(HD)


def place():
    s, h = lax.axis_index("seq"), lax.axis_index("head")
    return (s // 4) % 2 * 2 + h // 2, s % 4, s // 8, h % 2


def device(x, y, z, c):
    return (z * 8 + x // 2 * 4 + y, x % 2 * 2 + c)


def send(src, dst, ssem, rsem, to):
    return pltpu.make_async_remote_copy(
        src_ref=src, dst_ref=dst, send_sem=ssem, recv_sem=rsem, device_id=to, device_id_type=MESH
    )


def window_kernel(
    q_hbm, k_hbm, v_hbm, res_hbm, ctx_hbm, wa_hbm, wb_hbm, ga_hbm, gb_hbm, mixed_out, cache_out,
    q_in, k_in, v_in, res, wa, ga, gb,
    q_pack, kv_pack, kvm_pack, q_buf, kv, kvm, m_ref, l_ref, ot, o_buf, st_buf, o_rcv, m_rcv, st_rcv, stm_rcv, c_res, m_res, attn,
    w_all, ctx, b_part, b_rcv1, b_snd2, b_keep, b_rcv2, b_snd3, b_rcvx, b_rcv3, base,
    a_rows, p_pre, p_snd1, p_keep1, p_rcv1, p_snd2, p_rcv2,
    in_sem, xs_sem, xr_sem, ys_sem, yr_sem, zs_sem, zr_sem, os_sem, or_sem, bs_sem, br_sem,
    ws_sem, wr_sem, cs_sem, cr_sem, ds_sem, dr_sem, ps_sem, pr_sem,
):
    x, y, z, c = place()
    me = x * 2 + c
    xl, xh = x % 2, x // 2
    up, down = device(x, y, (z + 1) % 8, c), device(x, y, (z + 7) % 8, c)
    core_dev, pair_dev = device(x, y, z, 1 - c), device(xh * 2 + 1 - xl, y, z, c)
    far_x = (1 - xh) * 2 + xl
    x_peer = [None] + [(me + d) % 8 for d in range(1, 8)]
    x_dev = [None] + [device(p // 2, y, z, p % 2) for p in x_peer[1:]]
    sent = []

    def go(cp):
        cp.start()
        sent.append(cp)
        return cp

    loads = []
    for i, (src, dst) in enumerate((
        (k_hbm, k_in), (v_hbm, v_in), (q_hbm, q_in), (wb_hbm, w_all.at[z]), (ctx_hbm, ctx.at[0, 0]),
        (gb_hbm, gb), (res_hbm, res), (ga_hbm, ga), (wa_hbm, wa),
    )):
        loads.append(pltpu.make_async_copy(src, dst, in_sem.at[i]))
        if i < 8:
            loads[-1].start()

    barrier = pltpu.get_barrier_semaphore()
    peers = x_dev[1:] + [up, down]
    for d in range(1, 4):
        for cc in range(2):
            peers.append(device(x, (y + d) % 4, z, cc))
    for p in peers:
        pl.semaphore_signal(barrier, inc=1, device_id=p, device_id_type=MESH)

    for cp in loads[0:3]:
        cp.wait()
    for p in range(8):
        xx, cc = p // 2, p % 2
        heads = (5 * xx + 3 * cc, 5 * xx + 3 * cc + 1, 5 * xx + 2)
        for i, hh in enumerate(heads):
            cols = slice(hh * HD, (hh + 1) * HD)
            q_pack[p, i] = q_in[:, cols]
            if i < 2:
                kv_pack[p, i, 0] = k_in[:, cols]
                kv_pack[p, i, 1] = v_in[:, cols]
            elif cc == 0:
                kvm_pack[xx, 0] = k_in[:, cols]
                kvm_pack[xx, 1] = v_in[:, cols]
    q_buf[0, :, me] = q_pack[me]
    kv[0, :, me] = kv_pack[me]
    kvm[0, x] = kvm_pack[x]
    pl.semaphore_wait(barrier, len(peers))


    x_kv = [[], [], []]
    for i in range(2):
        for d in range(1, 8):
            x_kv[i].append(go(send(
                kv_pack.at[x_peer[d], i], kv.at[0, i, me], xs_sem.at[1 + i, d], xr_sem.at[1 + i, d], x_dev[d])))
    for d in range(1, 4):
        xx = (x + d) % 4
        x_kv[2].append(go(send(
            kvm_pack.at[xx], kvm.at[0, x], xs_sem.at[3, d], xr_sem.at[3, d], device(xx, y, z, c))))
    loads[8].start()
    x_q = []
    for d in range(1, 8):
        x_q.append(go(send(q_pack.at[x_peer[d]], q_buf.at[0, :, me], xs_sem.at[0, d], xr_sem.at[0, d], x_dev[d])))

    def w_ring(step, way):
        at = (z + 9 - step) % 8 if way == 0 else (z + 7 + step) % 8
        ref = w_all.at[at]
        if step == 4:
            ref = ref.at[0:48] if way == 0 else ref.at[48:80]
        return send(ref, ref, ws_sem.at[step, way], wr_sem.at[step, way], (up, down)[way])

    rings = {}

    def w_start(step):
        for way in range(2):
            rings[step, way] = go(w_ring(step, way))

    def w_wait(step):
        for way in range(2):
            rings[step, way].wait_recv()

    loads[3].wait()
    w_start(1)

    ctx_y = []
    loads[4].wait()
    for d in range(1, 4):
        ctx_y.append(go(send(ctx.at[0, 0], ctx.at[d, 0], cs_sem.at[d], cr_sem.at[d], device(x, (y + d) % 4, z, c))))
    w_wait(1)
    w_start(2)

    def part_ref(part, slot):
        return kvm.at[slot] if part == 2 else kv.at[slot, part]

    def ring(part, step, way):
        src = 0 if step == 1 else 2 * (step - 1) - 1 + way
        dst = 7 if step == 4 else 2 * step - 1 + way
        return send(
            part_ref(part, src), part_ref(part, dst), zs_sem.at[part, step, way], zr_sem.at[part, step, way], (up, down)[way])

    def ways_of(part, step):
        return (0, 1) if step < 4 else ((0,) if part == 0 else (1,))

    def ring_start(part, step):
        for way in ways_of(part, step):
            rings[part, step, way] = go(ring(part, step, way))

    def ring_next(part, step):
        for way in ways_of(part, step):
            rings[part, step, way].wait_recv()
        if step < 4:
            ring_start(part, step + 1)

    for part in range(3):
        for cp in x_kv[part]:
            cp.wait_recv()
        ring_start(part, 1)

    for cp in x_q:
        cp.wait_recv()
    y_q = []
    for d in range(1, 4):
        y_q.append(go(send(q_buf.at[0], q_buf.at[d], ys_sem.at[d], yr_sem.at[d], device(x, (y + d) % 4, z, c))))
    ctx_x = []
    for d in range(4):
        if d > 0:
            ctx_y[d - 1].wait_recv()
        ctx_x.append(go(send(ctx.at[d, 0], ctx.at[d, 1], cs_sem.at[4 + d], cr_sem.at[4 + d], device(far_x, y, z, c))))
    w_wait(2)
    w_start(3)

    def attend(head, lo, n, first=False, last=False):
        if head < 2:
            kk = kv[lo:lo + n, head, :, 0].reshape(n * 256, HD)
            vv = kv[lo:lo + n, head, :, 1].reshape(n * 256, HD)
        else:
            kk = kvm[lo:lo + n, :, 0].reshape(n * 128, HD)
            vv = kvm[lo:lo + n, :, 1].reshape(n * 128, HD)

        def scores(t):
            return lax.dot_general(
                kk, q_buf[t, head].reshape(256, HD), (((1,), (1,)), ((), ())), preferred_element_type=F32)

        def rest(t, s):
            top = jnp.max(s, axis=0, keepdims=True)
            if not first:
                old = m_ref[head, t]
                top = jnp.maximum(top, old)
                fade = jnp.exp2((old - top) * EXP2_SCALE)
            p = jnp.exp2(s * EXP2_SCALE - top * EXP2_SCALE)
            tot = jnp.sum(p, axis=0, keepdims=True)
            o = lax.dot_general(vv, p.astype(BF), (((0,), (0,)), ((), ())), preferred_element_type=F32)
            if not first:
                tot = l_ref[head, t] * fade + tot
                o = ot[head, t] * fade + o
            if last:
                o = (o * (1.0 / tot)).astype(BF)
                lse = top * EXP2_SCALE + jnp.log2(tot)
                for half in range(2):
                    cols = slice(half * HD, (half + 1) * HD)
                    o_buf[t, head, half] = o[:, cols]
                    st_buf[t, head, half, 0:1] = lse[:, cols]
            else:
                l_ref[head, t] = tot
                ot[head, t] = o
                m_ref[head, t] = top

        order = (1, 2, 3, 0)
        following = scores(order[0])
        for i, t in enumerate(order):
            current = following
            if i < 3:
                following = scores(order[i + 1])
            rest(t, current)

    for part in range(3):
        ring_next(part, 1)
    w_wait(3)
    w_start(4)
    for cp in y_q:
        cp.wait_recv()

    for part in range(3):
        attend(part, 0, 1, first=True)
    for part in range(3):
        ring_next(part, 2)
        attend(part, 1, 2)

    w_wait(4)
    for cp in ctx_x:
        cp.wait_recv()

    def b_tile(d, _):
        part = lax.dot_general(
            ctx[d].reshape(256, 640), w_all[...].reshape(640, 640),
            (((1,), (1,)), ((), ())), preferred_element_type=F32,
        )
        b_part[d] = part.astype(BF).reshape(2, 2, 2, 32, 640)
        return 0
    lax.fori_loop(0, 4, b_tile, 0)
    b_core = go(send(b_part.at[:, :, :, 1 - c], b_rcv1, ds_sem.at[0], dr_sem.at[0], core_dev))
    attend(0, 3, 2)
    ring_next(0, 3)
    attend(1, 3, 2)
    ring_next(1, 3)
    attend(2, 3, 2)
    ring_next(2, 3)
    b_core.wait_recv()

    def b_sum1(d, _):
        for e in range(2):
            b_snd2[e, d] = (b_part[d, e, 1 - xl, c].astype(F32) + b_rcv1[d, e, 1 - xl].astype(F32)).astype(BF)
            b_keep[e, d] = b_part[d, e, xl, c].astype(F32) + b_rcv1[d, e, xl].astype(F32)
        return 0
    lax.fori_loop(0, 4, b_sum1, 0)
    b_pair = go(send(b_snd2, b_rcv2, ds_sem.at[1], dr_sem.at[1], pair_dev))
    for part in range(3):
        attend(part, 5, 2)

    outs = [[], [], []]
    for head in range(3):
        ring_next(head, 4)
        attend(head, 7, 1, last=True)
        for t in (1, 2, 3, 0):
            yy = (y + 4 - t) % 4
            same, other = device(x, yy, z, c), device(x, yy, z, 1 - c)

            def out(src, dst, i, to):
                outs[head].append(go(send(src, dst, os_sem.at[t, i], or_sem.at[t, i], to)))

            if head < 2 and t > 0:
                out(o_buf.at[t, head], o_rcv.at[t, head], 2 * head, same)
                out(st_buf.at[t, head], st_rcv.at[t, head], 2 * head + 1, same)
            elif head == 2:
                if t > 0:
                    out(o_buf.at[t, 2, c], m_rcv.at[t, 0], 4, same)
                    out(st_buf.at[t, 2, c], stm_rcv.at[t, 0], 5, same)
                out(o_buf.at[t, 2, 1 - c], m_rcv.at[t, 1], 6, other)
                out(st_buf.at[t, 2, 1 - c], stm_rcv.at[t, 1], 7, other)

    b_pair.wait_recv()

    def b_sum2(d, _):
        for e in range(2):
            b_snd3[e, d] = (b_keep[e, d] + b_rcv2[e, d].astype(F32)).astype(BF)
        return 0
    lax.fori_loop(0, 4, b_sum2, 0)
    b_x = go(send(b_snd3.at[1], b_rcvx, ds_sem.at[2], dr_sem.at[2], device(far_x, y, z, c)))

    def merge(parts):
        top = parts[0][1]
        for _, s in parts[1:]:
            top = jnp.maximum(top, s)
        acc, tot = 0.0, 0.0
        for o, s in parts:
            w = jnp.exp2(s - top)
            acc = acc + o.astype(F32) * w
            tot = tot + w
        return (acc * (1.0 / tot)).T.astype(BF)

    back = []

    def give(src, head, sem, to_x, rsem):
        own = (to_x == x) & (x % 2 == c)
        cp = send(src, attn.at[head], bs_sem.at[sem], br_sem.at[rsem], device(to_x, y, z, x % 2))
        loc = pltpu.make_async_copy(src, attn.at[head], br_sem.at[rsem])

        @pl.when(own)
        def _():
            loc.start()

        @pl.when(jnp.logical_not(own))
        def _():
            cp.start()
        back.append((own, cp))

    for head in range(2):
        for cp in outs[head]:
            cp.wait_recv()
        for half in range(2):
            parts = [(o_buf[0, head, half], st_buf[0, head, half, 0:1])]
            for d in range(1, 4):
                parts.append((o_rcv[d, head, half], st_rcv[d, head, half, 0:1]))
            c_res[head, half] = merge(parts)
            give(c_res.at[head, half], 3 * c + head, 2 * head + half, 2 * half + x // 2, 3 * c + head)
    for cp in outs[2]:
        cp.wait_recv()
    parts = [(o_buf[0, 2, c], st_buf[0, 2, c, 0:1])]
    for d in range(4):
        if d > 0:
            parts.append((m_rcv[d, 0], stm_rcv[d, 0, 0:1]))
        parts.append((m_rcv[d, 1], stm_rcv[d, 1, 0:1]))
    m_res[...] = merge(parts)
    give(m_res, 2, 4, 2 * c + x // 2, 2)

    b_x.wait_recv()
    q_me, q_far = xh * 4 + y, (1 - xh) * 4 + y
    b_out = []
    for d in range(1, 4):
        to = device(x, (y + 4 - d) % 4, z, c)
        b_out.append(go(send(b_snd3.at[0, d], b_rcv3.at[q_me], ds_sem.at[2 + d], dr_sem.at[2 + d], to)))
        b_out.append(go(send(b_rcvx.at[d], b_rcv3.at[q_far], ds_sem.at[5 + d], dr_sem.at[5 + d], to)))
    b_rcv3[q_me] = b_snd3[0, 0]
    b_rcv3[q_far] = b_rcvx[0]

    def take(head):
        pltpu.make_async_copy(m_res, attn.at[head], br_sem.at[head]).wait()
        cache_out[:, head * HD:(head + 1) * HD] = attn[head]
        for i, (row_x, row_c) in enumerate(((1 - xl, 1 - c), (xl, 1 - c), (1 - xl, c), (xl, c))):
            a_rows[i * 32:(i + 1) * 32, head * HD:(head + 1) * HD] = attn[head, pl.ds((row_x * 2 + row_c) * 32, 32)]

    for head in (0, 1, 3, 4):
        take(head)
    loads[8].wait()
    for j in range(5):
        cols = slice(j * 1024, (j + 1) * 1024)
        p_pre[:, cols] = (
            jnp.dot(a_rows[:, 0:256], wa[0:256, cols], preferred_element_type=F32)
            + jnp.dot(a_rows[:, 384:640], wa[384:640, cols], preferred_element_type=F32)
        )
    take(2)
    stage1, stage2 = [], []
    for j in range(5):
        cols = slice(j * 1024, (j + 1) * 1024)
        part = jnp.dot(a_rows[:, 256:384], wa[256:384, cols], preferred_element_type=F32) + p_pre[:, cols]
        p_snd1[j] = part[0:64].astype(BF)
        stage1.append(go(send(p_snd1.at[j], p_rcv1.at[j], ps_sem.at[0, j], pr_sem.at[0, j], core_dev)))
        p_keep1[j] = part[64:128]
    for j in range(5):
        stage1[j].wait_recv()
        p_snd2[j] = (p_keep1[j, 0:32] + p_rcv1[j, 0:32].astype(F32)).astype(BF)
        stage2.append(go(send(p_snd2.at[j], p_rcv2.at[j], ps_sem.at[1, j], pr_sem.at[1, j], pair_dev)))

    for cp in b_out:
        cp.wait_recv()
    for cp in loads[5:8]:
        cp.wait()
    for zz in range(8):
        cols = slice(zz * 640, (zz + 1) * 640)
        piece = jnp.concatenate([b_rcv3[qq, :, zz * 80:(zz + 1) * 80].astype(F32) for qq in range(8)], axis=1)
        base[:, cols] = res[:, cols].astype(F32) + gb[:, cols] * piece
    for j in range(5):
        cols = slice(j * 1024, (j + 1) * 1024)
        stage2[j].wait_recv()
        total = p_keep1[j, 32:64] + p_rcv1[j, 32:64].astype(F32) + p_rcv2[j].astype(F32)
        mixed_out[:, cols] = (base[:, cols] + ga[:, cols] * total).astype(BF)

    for cp in sent:
        cp.wait_send()
    for own, cp in back:
        @pl.when(jnp.logical_not(own))
        def _():
            cp.wait_send()


def window(q, k, v, res, ctx, wa, wb, ga, gb):
    any_space = pl.BlockSpec(memory_space=pl.ANY)
    vm = pl.BlockSpec(memory_space=pltpu.VMEM)
    D = pltpu.SemaphoreType.DMA
    V = pltpu.VMEM
    return pl.pallas_call(
        window_kernel,
        out_shape=(jax.ShapeDtypeStruct((32, 5120), BF), jax.ShapeDtypeStruct((128, 640), BF)),
        in_specs=[any_space] * 9,
        out_specs=(vm, vm),
        scratch_shapes=[
            V((32, 2560), BF), V((32, 2560), BF), V((32, 2560), BF), V((32, 5120), BF),
            V((640, 5120), BF), V((1, 5120), F32), V((1, 5120), F32),
            V((8, 3, 32, HD), BF), V((8, 2, 2, 32, HD), BF), V((4, 2, 32, HD), BF),
            V((4, 3, 8, 32, HD), BF),
            V((8, 2, 8, 2, 32, HD), BF), V((8, 4, 2, 32, HD), BF),
            V((3, 4, 1, 256), F32), V((3, 4, 1, 256), F32), V((3, 4, HD, 256), F32),
            V((4, 3, 2, HD, HD), BF), V((4, 3, 2, 8, HD), F32),
            V((4, 2, 2, HD, HD), BF), V((4, 2, HD, HD), BF), V((4, 2, 2, 8, HD), F32), V((4, 2, 8, HD), F32),
            V((2, 2, HD, HD), BF), V((HD, HD), BF), V((5, HD, HD), BF),
            V((8, 80, 640), BF), V((4, 2, HD, 640), BF), V((4, 2, 2, 2, 32, 640), BF), V((4, 2, 2, 32, 640), BF),
            V((2, 4, 32, 640), BF), V((2, 4, 32, 640), F32), V((2, 4, 32, 640), BF), V((2, 4, 32, 640), BF), V((4, 32, 640), BF),
            V((8, 32, 640), BF), V((32, 5120), F32),
            V((HD, 640), BF), V((HD, 5120), F32), V((5, 64, 1024), BF), V((5, 64, 1024), F32), V((5, 64, 1024), BF),
            V((5, 32, 1024), BF), V((5, 32, 1024), BF),
            D((9,)), D((4, 8)), D((4, 8)), D((4,)), D((4,)), D((3, 5, 2)), D((3, 5, 2)), D((4, 8)), D((4, 8)),
            D((5,)), D((5,)), D((5, 2)), D((5, 2)), D((8,)), D((8,)), D((9,)), D((9,)), D((2, 5)), D((2, 5)),
        ],
        compiler_params=pltpu.CompilerParams(collective_id=1, has_side_effects=True, vmem_limit_bytes=56 * 2**20),
        name="window",
    )(q, k, v, res, ctx, wa, wb.T, ga.reshape(1, 5120), gb.reshape(1, 5120))


def finish_kernel(mixed_in, cache_in, mixed_out, cache_out):
    mixed_out[...] = mixed_in[...]
    cache_out[...] = cache_in[...]


def finish(mixed, cache):
    vm = pl.BlockSpec(memory_space=pltpu.VMEM)
    return pl.pallas_call(
        finish_kernel,
        out_shape=(jax.ShapeDtypeStruct(mixed.shape, BF), jax.ShapeDtypeStruct(cache.shape, BF)),
        in_specs=[vm] * 2,
        out_specs=(vm, vm),
        name="finish",
    )(mixed, cache)


def on_device(*arrays):
    out = window(*arrays)
    return finish(*out)


def solution(mesh):
    tokens = P(("seq", "head"), None)
    return jax.shard_map(
        on_device,
        mesh=mesh,
        in_specs=(tokens, tokens, tokens, tokens, P("seq", "head"), P("head", None), P("head", "seq"), P(), P()),
        out_specs=(tokens, P("seq", "head")),
        check_vma=False,
    )
```

time: 103 us -> 76.2 us (0.74)
  Pallas kernels: 97.1 us -> 75.5 us
  local copies, waits for them, and re-layouts: 5.01 us -> 0 us
    pallas_call x1, Pallas kernels: 97.1 us -> 73.6 us  [window(): pl.pallas_call(window_kernel, out_shape=(jax.ShapeDtypeStruct((32, 5120),...]
    unnamed x3 -> x0, local copies, waits for them, and re-layouts: 5.01 us -> none
    pallas_call x0 -> x1, Pallas kernels: none -> 1.81 us  [finish(): pl.pallas_call(finish_kernel, out_shape=(jax.ShapeDtypeStruct(mixed.shape...]
where the time goes in v3:
time: 76.2 us; the launch traced here: 76.1 us
  Pallas kernels  75.5 us (99%)
    pallas_call x1, Pallas kernels, window(): pl.pallas_call(window_kernel, out_shape=(jax.ShapeDtypeStruct((32, 5120),...  73.6 us
    pallas_call x1, Pallas kernels, finish(): pl.pallas_call(finish_kernel, out_shape=(jax.ShapeDtypeStruct(mixed.shape...  1.81 us

profile of v3, /device:TPU:1, one launch (start us, length us, event | category | flops | bytes accessed | tf_op | source)
XLA Modules:
  0.0 76.1 jit_solution(15263657428672322674)
XLA Ops:
  0.6 73.6 %window.1 = (bf16[32,5120]{1,0:T(8,128)(2,1)}, bf16[128,640]{1,0:T(8,128)(2,1)}) custom-call(bf16[32,2560]{1,0:T(8,128)(2,1)} %q_hbm.1, bf16[32,2560]{1,0:T(8,128)(2,1)} %k_hbm.1, bf16[32,2560]{1,0:T(8,128)(2,1)} %v_hbm.1, bf16[32,5120]{1,0:T(8,128)(2,1)} %res_hbm.1, bf16[128,640]{1,0:T(8,128)(2,1)} %ctx_hbm.1, bf16[640,5120]{1,0:T(8,128)(2,1)} %wa_hbm.1, ...), custom_call_target="tpu_custom_call" | custom-call | tf_op jit(solution)/shard_map/window/pallas_call | solution.py:403
  74.3 1.8 %finish.1 = (bf16[32,5120]{1,0:T(8,128)(2,1)}, bf16[128,640]{1,0:T(8,128)(2,1)}) custom-call(bf16[32,5120]{1,0:T(8,128)(2,1)} %get-tuple-element.4.mixed_in, bf16[128,640]{1,0:T(8,128)(2,1)} %get-tuple-element.5.cache_in), custom_call_target="tpu_custom_call" | custom-call | tf_op jit(solution)/shard_map/finish/pallas_call | solution.py:438

commit v4 on v3

--- a/solution.py
+++ b/solution.py
@@ -32,7 +32,7 @@
 def window_kernel(
     q_hbm, k_hbm, v_hbm, res_hbm, ctx_hbm, wa_hbm, wb_hbm, ga_hbm, gb_hbm, mixed_out, cache_out,
     q_in, k_in, v_in, res, wa, ga, gb,
-    q_pack, kv_pack, kvm_pack, q_buf, kv, kvm, m_ref, l_ref, ot, o_buf, st_buf, o_rcv, m_rcv, st_rcv, stm_rcv, c_res, m_res, attn,
+    q_pack, kv_pack, kvm_pack, q_buf, kv, kvm, m_ref, l_ref, ot, o_buf, st_buf, o_rcv, m_rcv, st_rcv, stm_rcv, c_res, m_res, attn, attn_far,
     w_all, ctx, b_part, b_rcv1, b_snd2, b_keep, b_rcv2, b_snd3, b_rcvx, b_rcv3, base,
     a_rows, p_pre, p_snd1, p_keep1, p_rcv1, p_snd2, p_rcv2,
     in_sem, xs_sem, xr_sem, ys_sem, yr_sem, zs_sem, zr_sem, os_sem, or_sem, bs_sem, br_sem,
@@ -89,6 +89,31 @@
     kvm[0, x] = kvm_pack[x]
     pl.semaphore_wait(barrier, len(peers))
 
+    def w_ring(step, way):
+        at = (z + 9 - step) % 8 if way == 0 else (z + 7 + step) % 8
+        ref = w_all.at[at]
+        if step == 4:
+            ref = ref.at[0:48] if way == 0 else ref.at[48:80]
+        return send(ref, ref, ws_sem.at[step, way], wr_sem.at[step, way], (up, down)[way])
+
+    rings = {}
+
+    def w_start(step):
+        for way in range(2):
+            rings[step, way] = go(w_ring(step, way))
+
+    def w_wait(step):
+        for way in range(2):
+            rings[step, way].wait_recv()
+
+    loads[3].wait()
+    w_start(1)
+
+    x_q = []
+
+    def send_q():
+        for d in range(1, 8):
+            x_q.append(go(send(q_pack.at[x_peer[d]], q_buf.at[0, :, me], xs_sem.at[0, d], xr_sem.at[0, d], x_dev[d])))
 
     x_kv = [[], [], []]
     for i in range(2):
@@ -100,34 +125,11 @@
         x_kv[2].append(go(send(
             kvm_pack.at[xx], kvm.at[0, x], xs_sem.at[3, d], xr_sem.at[3, d], device(xx, y, z, c))))
     loads[8].start()
-    x_q = []
-    for d in range(1, 8):
-        x_q.append(go(send(q_pack.at[x_peer[d]], q_buf.at[0, :, me], xs_sem.at[0, d], xr_sem.at[0, d], x_dev[d])))
-
-    def w_ring(step, way):
-        at = (z + 9 - step) % 8 if way == 0 else (z + 7 + step) % 8
-        ref = w_all.at[at]
-        if step == 4:
-            ref = ref.at[0:48] if way == 0 else ref.at[48:80]
-        return send(ref, ref, ws_sem.at[step, way], wr_sem.at[step, way], (up, down)[way])
-
-    rings = {}
-
-    def w_start(step):
-        for way in range(2):
-            rings[step, way] = go(w_ring(step, way))
-
-    def w_wait(step):
-        for way in range(2):
-            rings[step, way].wait_recv()
-
-    loads[3].wait()
-    w_start(1)
-
+    send_q()
     ctx_y = []
     loads[4].wait()
     for d in range(1, 4):
-        ctx_y.append(go(send(ctx.at[0, 0], ctx.at[d, 0], cs_sem.at[d], cr_sem.at[d], device(x, (y + d) % 4, z, c))))
+        ctx_y.append(go(send(ctx.at[0, 0], ctx.at[0, d], cs_sem.at[d], cr_sem.at[d], device(x, (y + d) % 4, z, c))))
     w_wait(1)
     w_start(2)
 
@@ -167,7 +169,7 @@
     for d in range(4):
         if d > 0:
             ctx_y[d - 1].wait_recv()
-        ctx_x.append(go(send(ctx.at[d, 0], ctx.at[d, 1], cs_sem.at[4 + d], cr_sem.at[4 + d], device(far_x, y, z, c))))
+        ctx_x.append(go(send(ctx.at[0, d], ctx.at[1, d], cs_sem.at[4 + d], cr_sem.at[4 + d], device(far_x, y, z, c))))
     w_wait(2)
     w_start(3)
 
@@ -215,49 +217,58 @@
                 following = scores(order[i + 1])
             rest(t, current)
 
-    for part in range(3):
-        ring_next(part, 1)
+    b_core, b_pair = [], []
+
+    def b_dot(e):
+        def tile(i, _):
+            part = lax.dot_general(
+                ctx[e, pl.ds(2 * i, 2)].reshape(256, 640), w_all[...].reshape(640, 640),
+                (((1,), (1,)), ((), ())), preferred_element_type=F32,
+            )
+            b_part[e, pl.ds(2 * i, 2)] = part.astype(BF).reshape(2, 2, 2, 32, 640)
+            return 0
+        lax.fori_loop(0, 2, tile, 0)
+        b_core.append(go(send(b_part.at[e, :, :, 1 - c], b_rcv1.at[e], ds_sem.at[e], dr_sem.at[e], core_dev)))
+
+    def b_sum1(e):
+        b_core[e].wait_recv()
+
+        def tile(d, _):
+            b_snd2[e, d] = (b_part[e, d, 1 - xl, c].astype(F32) + b_rcv1[e, d, 1 - xl].astype(F32)).astype(BF)
+            b_keep[e, d] = b_part[e, d, xl, c].astype(F32) + b_rcv1[e, d, xl].astype(F32)
+            return 0
+        lax.fori_loop(0, 4, tile, 0)
+        b_pair.append(go(send(b_snd2.at[e], b_rcv2.at[e], ds_sem.at[2 + e], dr_sem.at[2 + e], pair_dev)))
+
+    ring_next(0, 1)
     w_wait(3)
     w_start(4)
+    ring_next(1, 1)
+    ring_next(2, 1)
+    w_wait(4)
+    b_dot(0)
+    ring_next(0, 2)
     for cp in y_q:
         cp.wait_recv()
-
-    for part in range(3):
-        attend(part, 0, 1, first=True)
-    for part in range(3):
-        ring_next(part, 2)
-        attend(part, 1, 2)
-
-    w_wait(4)
+    attend(0, 0, 3, first=True)
+    ring_next(1, 2)
+    attend(1, 0, 3, first=True)
+    ring_next(2, 2)
+    attend(2, 0, 3, first=True)
+    b_sum1(0)
+    attend(0, 3, 2)
     for cp in ctx_x:
         cp.wait_recv()
-
-    def b_tile(d, _):
-        part = lax.dot_general(
-            ctx[d].reshape(256, 640), w_all[...].reshape(640, 640),
-            (((1,), (1,)), ((), ())), preferred_element_type=F32,
-        )
-        b_part[d] = part.astype(BF).reshape(2, 2, 2, 32, 640)
-        return 0
-    lax.fori_loop(0, 4, b_tile, 0)
-    b_core = go(send(b_part.at[:, :, :, 1 - c], b_rcv1, ds_sem.at[0], dr_sem.at[0], core_dev))
-    attend(0, 3, 2)
+    b_dot(1)
     ring_next(0, 3)
     attend(1, 3, 2)
     ring_next(1, 3)
     attend(2, 3, 2)
     ring_next(2, 3)
-    b_core.wait_recv()
-
-    def b_sum1(d, _):
-        for e in range(2):
-            b_snd2[e, d] = (b_part[d, e, 1 - xl, c].astype(F32) + b_rcv1[d, e, 1 - xl].astype(F32)).astype(BF)
-            b_keep[e, d] = b_part[d, e, xl, c].astype(F32) + b_rcv1[d, e, xl].astype(F32)
-        return 0
-    lax.fori_loop(0, 4, b_sum1, 0)
-    b_pair = go(send(b_snd2, b_rcv2, ds_sem.at[1], dr_sem.at[1], pair_dev))
-    for part in range(3):
-        attend(part, 5, 2)
+    attend(0, 5, 2)
+    b_sum1(1)
+    attend(1, 5, 2)
+    attend(2, 5, 2)
 
     outs = [[], [], []]
     for head in range(3):
@@ -280,14 +291,15 @@
                 out(o_buf.at[t, 2, 1 - c], m_rcv.at[t, 1], 6, other)
                 out(st_buf.at[t, 2, 1 - c], stm_rcv.at[t, 1], 7, other)
 
-    b_pair.wait_recv()
+    for e in range(2):
+        b_pair[e].wait_recv()
 
     def b_sum2(d, _):
         for e in range(2):
             b_snd3[e, d] = (b_keep[e, d] + b_rcv2[e, d].astype(F32)).astype(BF)
         return 0
     lax.fori_loop(0, 4, b_sum2, 0)
-    b_x = go(send(b_snd3.at[1], b_rcvx, ds_sem.at[2], dr_sem.at[2], device(far_x, y, z, c)))
+    b_x = go(send(b_snd3.at[1], b_rcvx, ds_sem.at[4], dr_sem.at[4], device(far_x, y, z, c)))
 
     def merge(parts):
         top = parts[0][1]
@@ -302,10 +314,10 @@
 
     back = []
 
-    def give(src, head, sem, to_x, rsem):
+    def give(src, dst, sem, to_x, rsem):
         own = (to_x == x) & (x % 2 == c)
-        cp = send(src, attn.at[head], bs_sem.at[sem], br_sem.at[rsem], device(to_x, y, z, x % 2))
-        loc = pltpu.make_async_copy(src, attn.at[head], br_sem.at[rsem])
+        cp = send(src, dst, bs_sem.at[sem], br_sem.at[rsem], device(to_x, y, z, x % 2))
+        loc = pltpu.make_async_copy(src, dst, br_sem.at[rsem])
 
         @pl.when(own)
         def _():
@@ -315,6 +327,10 @@
         def _():
             cp.start()
         back.append((own, cp))
+
+    def give_rows(src, head, sem, half):
+        give(src, attn.at[head], sem, 2 * half + x // 2, head)
+        give(src.at[1 - x // 2, :, 1], attn_far.at[head], 5 + sem, 2 * (1 - half) + x // 2, 5 + head)
 
     for head in range(2):
         for cp in outs[head]:
@@ -323,8 +339,8 @@
             parts = [(o_buf[0, head, half], st_buf[0, head, half, 0:1])]
             for d in range(1, 4):
                 parts.append((o_rcv[d, head, half], st_rcv[d, head, half, 0:1]))
-            c_res[head, half] = merge(parts)
-            give(c_res.at[head, half], 3 * c + head, 2 * head + half, 2 * half + x // 2, 3 * c + head)
+            c_res[head, half] = merge(parts).reshape(2, 2, 2, 16, HD)
+            give_rows(c_res.at[head, half], 3 * c + head, 2 * head + half, half)
     for cp in outs[2]:
         cp.wait_recv()
     parts = [(o_buf[0, 2, c], st_buf[0, 2, c, 0:1])]
@@ -332,24 +348,28 @@
         if d > 0:
             parts.append((m_rcv[d, 0], stm_rcv[d, 0, 0:1]))
         parts.append((m_rcv[d, 1], stm_rcv[d, 1, 0:1]))
-    m_res[...] = merge(parts)
-    give(m_res, 2, 4, 2 * c + x // 2, 2)
+    m_res[...] = merge(parts).reshape(2, 2, 2, 16, HD)
+    give_rows(m_res, 2, 4, c)
 
     b_x.wait_recv()
     q_me, q_far = xh * 4 + y, (1 - xh) * 4 + y
     b_out = []
     for d in range(1, 4):
         to = device(x, (y + 4 - d) % 4, z, c)
-        b_out.append(go(send(b_snd3.at[0, d], b_rcv3.at[q_me], ds_sem.at[2 + d], dr_sem.at[2 + d], to)))
-        b_out.append(go(send(b_rcvx.at[d], b_rcv3.at[q_far], ds_sem.at[5 + d], dr_sem.at[5 + d], to)))
+        b_out.append(go(send(b_snd3.at[0, d], b_rcv3.at[q_me], ds_sem.at[4 + d], dr_sem.at[4 + d], to)))
+        b_out.append(go(send(b_rcvx.at[d], b_rcv3.at[q_far], ds_sem.at[7 + d], dr_sem.at[7 + d], to)))
     b_rcv3[q_me] = b_snd3[0, 0]
     b_rcv3[q_far] = b_rcvx[0]
 
     def take(head):
         pltpu.make_async_copy(m_res, attn.at[head], br_sem.at[head]).wait()
-        cache_out[:, head * HD:(head + 1) * HD] = attn[head]
-        for i, (row_x, row_c) in enumerate(((1 - xl, 1 - c), (xl, 1 - c), (1 - xl, c), (xl, c))):
-            a_rows[i * 32:(i + 1) * 32, head * HD:(head + 1) * HD] = attn[head, pl.ds((row_x * 2 + row_c) * 32, 32)]
+        pltpu.make_async_copy(m_res.at[0, :, 1], attn_far.at[head], br_sem.at[5 + head]).wait()
+        cols = slice(head * HD, (head + 1) * HD)
+        cache_out[:, cols] = attn[head].reshape(HD, HD)
+        for i, row_c in enumerate((1 - c, c)):
+            a_rows[i * 64:i * 64 + 32, cols] = attn[head, xl, row_c].reshape(32, HD)
+            a_rows[i * 64 + 32:i * 64 + 48, cols] = attn[head, 1 - xl, row_c, 0]
+            a_rows[i * 64 + 48:i * 64 + 64, cols] = attn_far[head, row_c]
 
     for head in (0, 1, 3, 4):
         take(head)
@@ -370,8 +390,9 @@
         p_keep1[j] = part[64:128]
     for j in range(5):
         stage1[j].wait_recv()
-        p_snd2[j] = (p_keep1[j, 0:32] + p_rcv1[j, 0:32].astype(F32)).astype(BF)
-        stage2.append(go(send(p_snd2.at[j], p_rcv2.at[j], ps_sem.at[1, j], pr_sem.at[1, j], pair_dev)))
+        p_snd2[j] = (p_keep1[j, 32:64] + p_rcv1[j, 32:64].astype(F32)).astype(BF).reshape(2, 16, 1024)
+        for i, to in enumerate((pair_dev, device(2 * (1 - xh) + 1 - xl, y, z, c))):
+            stage2.append(go(send(p_snd2.at[j, i], p_rcv2.at[j, i], ps_sem.at[1 + i, j], pr_sem.at[1 + i, j], to)))
 
     for cp in b_out:
         cp.wait_recv()
@@ -383,8 +404,9 @@
         base[:, cols] = res[:, cols].astype(F32) + gb[:, cols] * piece
     for j in range(5):
         cols = slice(j * 1024, (j + 1) * 1024)
-        stage2[j].wait_recv()
-        total = p_keep1[j, 32:64] + p_rcv1[j, 32:64].astype(F32) + p_rcv2[j].astype(F32)
+        for i in range(2):
+            stage2[2 * j + i].wait_recv()
+        total = p_keep1[j, 0:32] + p_rcv1[j, 0:32].astype(F32) + p_rcv2[j].reshape(32, 1024).astype(F32)
         mixed_out[:, cols] = (base[:, cols] + ga[:, cols] * total).astype(BF)
 
     for cp in sent:
@@ -414,14 +436,14 @@
             V((3, 4, 1, 256), F32), V((3, 4, 1, 256), F32), V((3, 4, HD, 256), F32),
             V((4, 3, 2, HD, HD), BF), V((4, 3, 2, 8, HD), F32),
             V((4, 2, 2, HD, HD), BF), V((4, 2, HD, HD), BF), V((4, 2, 2, 8, HD), F32), V((4, 2, 8, HD), F32),
-            V((2, 2, HD, HD), BF), V((HD, HD), BF), V((5, HD, HD), BF),
-            V((8, 80, 640), BF), V((4, 2, HD, 640), BF), V((4, 2, 2, 2, 32, 640), BF), V((4, 2, 2, 32, 640), BF),
+            V((2, 2, 2, 2, 2, 16, HD), BF), V((2, 2, 2, 16, HD), BF), V((5, 2, 2, 2, 16, HD), BF), V((5, 2, 16, HD), BF),
+            V((8, 80, 640), BF), V((2, 4, HD, 640), BF), V((2, 4, 2, 2, 32, 640), BF), V((2, 4, 2, 32, 640), BF),
             V((2, 4, 32, 640), BF), V((2, 4, 32, 640), F32), V((2, 4, 32, 640), BF), V((2, 4, 32, 640), BF), V((4, 32, 640), BF),
             V((8, 32, 640), BF), V((32, 5120), F32),
             V((HD, 640), BF), V((HD, 5120), F32), V((5, 64, 1024), BF), V((5, 64, 1024), F32), V((5, 64, 1024), BF),
-            V((5, 32, 1024), BF), V((5, 32, 1024), BF),
+            V((5, 2, 16, 1024), BF), V((5, 2, 16, 1024), BF),
             D((9,)), D((4, 8)), D((4, 8)), D((4,)), D((4,)), D((3, 5, 2)), D((3, 5, 2)), D((4, 8)), D((4, 8)),
-            D((5,)), D((5,)), D((5, 2)), D((5, 2)), D((8,)), D((8,)), D((9,)), D((9,)), D((2, 5)), D((2, 5)),
+            D((10,)), D((10,)), D((5, 2)), D((5, 2)), D((8,)), D((8,)), D((11,)), D((11,)), D((3, 5)), D((3, 5)),
         ],
         compiler_params=pltpu.CompilerParams(collective_id=1, has_side_effects=True, vmem_limit_bytes=56 * 2**20),
         name="window",

time: 76.2 us -> 73.2 us (0.961)
  Pallas kernels: 75.5 us -> 72.5 us
    pallas_call x1, Pallas kernels: 73.6 us -> 70.7 us  [window(): pl.pallas_call(window_kernel, out_shape=(jax.ShapeDtypeStruct((32, 5120),...]
where the time goes in v4:
time: 73.2 us; the launch traced here: 73.1 us
  Pallas kernels  72.5 us (99%)
    pallas_call x1, Pallas kernels, window(): pl.pallas_call(window_kernel, out_shape=(jax.ShapeDtypeStruct((32, 5120),...  70.7 us
    pallas_call x1, Pallas kernels, finish(): pl.pallas_call(finish_kernel, out_shape=(jax.ShapeDtypeStruct(mixed.shape...  1.81 us

profile of v4, /device:TPU:1, one launch (start us, length us, event | category | flops | bytes accessed | tf_op | source)
XLA Modules:
  0.0 73.1 jit_solution(13869811478117996462)
XLA Ops:
  0.6 70.7 %window.1 = (bf16[32,5120]{1,0:T(8,128)(2,1)}, bf16[128,640]{1,0:T(8,128)(2,1)}) custom-call(bf16[32,2560]{1,0:T(8,128)(2,1)} %q_hbm.1, bf16[32,2560]{1,0:T(8,128)(2,1)} %k_hbm.1, bf16[32,2560]{1,0:T(8,128)(2,1)} %v_hbm.1, bf16[32,5120]{1,0:T(8,128)(2,1)} %res_hbm.1, bf16[128,640]{1,0:T(8,128)(2,1)} %ctx_hbm.1, bf16[640,5120]{1,0:T(8,128)(2,1)} %wa_hbm.1, ...), custom_call_target="tpu_custom_call" | custom-call | tf_op jit(solution)/shard_map/window/pallas_call | solution.py:425
  71.3 1.8 %finish.1 = (bf16[32,5120]{1,0:T(8,128)(2,1)}, bf16[128,640]{1,0:T(8,128)(2,1)}) custom-call(bf16[32,5120]{1,0:T(8,128)(2,1)} %get-tuple-element.4.mixed_in, bf16[128,640]{1,0:T(8,128)(2,1)} %get-tuple-element.5.cache_in), custom_call_target="tpu_custom_call" | custom-call | tf_op jit(solution)/shard_map/finish/pallas_call | solution.py:460

commit v5 on v4

--- a/solution.py
+++ b/solution.py
@@ -450,18 +450,31 @@
     )(q, k, v, res, ctx, wa, wb.T, ga.reshape(1, 5120), gb.reshape(1, 5120))
 
 
-def finish_kernel(mixed_in, cache_in, mixed_out, cache_out):
-    mixed_out[...] = mixed_in[...]
-    cache_out[...] = cache_in[...]
+def finish_kernel(mixed_in, cache_in, mixed_out, cache_out, mixed, cache, in_sem, out_sem):
+    pieces = [(mixed_in.at[:, cols], mixed.at[:, cols], mixed_out.at[:, cols])
+              for cols in (slice(0, 2560), slice(2560, 5120))] + [(cache_in, cache, cache_out)]
+    reads = [pltpu.make_async_copy(src, mid, in_sem.at[i]) for i, (src, mid, _) in enumerate(pieces)]
+    writes = [pltpu.make_async_copy(mid, dst, out_sem.at[i]) for i, (_, mid, dst) in enumerate(pieces)]
+    for cp in reads:
+        cp.start()
+    for read, write in zip(reads, writes):
+        read.wait()
+        write.start()
+    for cp in writes:
+        cp.wait()
 
 
 def finish(mixed, cache):
-    vm = pl.BlockSpec(memory_space=pltpu.VMEM)
+    any_space = pl.BlockSpec(memory_space=pl.ANY)
     return pl.pallas_call(
         finish_kernel,
         out_shape=(jax.ShapeDtypeStruct(mixed.shape, BF), jax.ShapeDtypeStruct(cache.shape, BF)),
-        in_specs=[vm] * 2,
-        out_specs=(vm, vm),
+        in_specs=[any_space] * 2,
+        out_specs=(any_space, any_space),
+        scratch_shapes=[
+            pltpu.VMEM(mixed.shape, BF), pltpu.VMEM(cache.shape, BF),
+            pltpu.SemaphoreType.DMA((3,)), pltpu.SemaphoreType.DMA((3,)),
+        ],
         name="finish",
     )(mixed, cache)
 

time: 73.2 us -> 73.4 us (level)
  no operation moved by 1% of the time
where the time goes in v5:
time: 73.4 us; the launch traced here: 73.3 us
  Pallas kernels  72.5 us (99%)
  between operations  0.8 us (1%)
    pallas_call x1, Pallas kernels, window(): pl.pallas_call(window_kernel, out_shape=(jax.ShapeDtypeStruct((32, 5120),...  70.7 us
    pallas_call x1, Pallas kernels, finish(): pl.pallas_call(finish_kernel, out_shape=(jax.ShapeDtypeStruct(mixed.shape...  1.79 us

profile of v5, /device:TPU:1, one launch (start us, length us, event | category | flops | bytes accessed | tf_op | source)
XLA Modules:
  0.0 73.3 jit_solution(10698626027971332373)
XLA Ops:
  0.6 70.7 %window.1 = (bf16[32,5120]{1,0:T(8,128)(2,1)}, bf16[128,640]{1,0:T(8,128)(2,1)}) custom-call(bf16[32,2560]{1,0:T(8,128)(2,1)} %q_hbm.1, bf16[32,2560]{1,0:T(8,128)(2,1)} %k_hbm.1, bf16[32,2560]{1,0:T(8,128)(2,1)} %v_hbm.1, bf16[32,5120]{1,0:T(8,128)(2,1)} %res_hbm.1, bf16[128,640]{1,0:T(8,128)(2,1)} %ctx_hbm.1, bf16[640,5120]{1,0:T(8,128)(2,1)} %wa_hbm.1, ...), custom_call_target="tpu_custom_call" | custom-call | tf_op jit(solution)/shard_map/window/pallas_call | solution.py:425
  71.3 1.8 %finish.1 = (bf16[32,5120]{1,0:T(8,128)(2,1)}, bf16[128,640]{1,0:T(8,128)(2,1)}) custom-call(bf16[32,5120]{1,0:T(8,128)(2,1)} %get-tuple-element.4.mixed_in, bf16[128,640]{1,0:T(8,128)(2,1)} %get-tuple-element.5.cache_in), custom_call_target="tpu_custom_call" | custom-call | tf_op jit(solution)/shard_map/finish/pallas_call | solution.py:469

commit v6 on v4

--- a/solution.py
+++ b/solution.py
@@ -53,6 +53,14 @@
         sent.append(cp)
         return cp
 
+    barrier = pltpu.get_barrier_semaphore()
+    peers = x_dev[1:] + [up, down]
+    for d in range(1, 4):
+        for cc in range(2):
+            peers.append(device(x, (y + d) % 4, z, cc))
+    for p in peers:
+        pl.semaphore_signal(barrier, inc=1, device_id=p, device_id_type=MESH)
+
     loads = []
     for i, (src, dst) in enumerate((
         (k_hbm, k_in), (v_hbm, v_in), (q_hbm, q_in), (wb_hbm, w_all.at[z]), (ctx_hbm, ctx.at[0, 0]),
@@ -62,29 +70,19 @@
         if i < 8:
             loads[-1].start()
 
-    barrier = pltpu.get_barrier_semaphore()
-    peers = x_dev[1:] + [up, down]
-    for d in range(1, 4):
-        for cc in range(2):
-            peers.append(device(x, (y + d) % 4, z, cc))
-    for p in peers:
-        pl.semaphore_signal(barrier, inc=1, device_id=p, device_id_type=MESH)
-
-    for cp in loads[0:3]:
+    for cp in loads[0:2]:
         cp.wait()
     for p in range(8):
         xx, cc = p // 2, p % 2
         heads = (5 * xx + 3 * cc, 5 * xx + 3 * cc + 1, 5 * xx + 2)
         for i, hh in enumerate(heads):
             cols = slice(hh * HD, (hh + 1) * HD)
-            q_pack[p, i] = q_in[:, cols]
             if i < 2:
                 kv_pack[p, i, 0] = k_in[:, cols]
                 kv_pack[p, i, 1] = v_in[:, cols]
             elif cc == 0:
                 kvm_pack[xx, 0] = k_in[:, cols]
                 kvm_pack[xx, 1] = v_in[:, cols]
-    q_buf[0, :, me] = q_pack[me]
     kv[0, :, me] = kv_pack[me]
     kvm[0, x] = kvm_pack[x]
     pl.semaphore_wait(barrier, len(peers))
@@ -112,6 +110,12 @@
     x_q = []
 
     def send_q():
+        loads[2].wait()
+        for p in range(8):
+            xx, cc = p // 2, p % 2
+            for i, hh in enumerate((5 * xx + 3 * cc, 5 * xx + 3 * cc + 1, 5 * xx + 2)):
+                q_pack[p, i] = q_in[:, hh * HD:(hh + 1) * HD]
+        q_buf[0, :, me] = q_pack[me]
         for d in range(1, 8):
             x_q.append(go(send(q_pack.at[x_peer[d]], q_buf.at[0, :, me], xs_sem.at[0, d], xr_sem.at[0, d], x_dev[d])))
 
@@ -374,23 +378,23 @@
     for head in (0, 1, 3, 4):
         take(head)
     loads[8].wait()
-    for j in range(5):
-        cols = slice(j * 1024, (j + 1) * 1024)
+    for j in range(2):
+        cols = slice(j * 2560, (j + 1) * 2560)
         p_pre[:, cols] = (
             jnp.dot(a_rows[:, 0:256], wa[0:256, cols], preferred_element_type=F32)
             + jnp.dot(a_rows[:, 384:640], wa[384:640, cols], preferred_element_type=F32)
         )
     take(2)
     stage1, stage2 = [], []
-    for j in range(5):
-        cols = slice(j * 1024, (j + 1) * 1024)
+    for j in range(2):
+        cols = slice(j * 2560, (j + 1) * 2560)
         part = jnp.dot(a_rows[:, 256:384], wa[256:384, cols], preferred_element_type=F32) + p_pre[:, cols]
         p_snd1[j] = part[0:64].astype(BF)
         stage1.append(go(send(p_snd1.at[j], p_rcv1.at[j], ps_sem.at[0, j], pr_sem.at[0, j], core_dev)))
         p_keep1[j] = part[64:128]
-    for j in range(5):
+    for j in range(2):
         stage1[j].wait_recv()
-        p_snd2[j] = (p_keep1[j, 32:64] + p_rcv1[j, 32:64].astype(F32)).astype(BF).reshape(2, 16, 1024)
+        p_snd2[j] = (p_keep1[j, 32:64] + p_rcv1[j, 32:64].astype(F32)).astype(BF).reshape(2, 16, 2560)
         for i, to in enumerate((pair_dev, device(2 * (1 - xh) + 1 - xl, y, z, c))):
             stage2.append(go(send(p_snd2.at[j, i], p_rcv2.at[j, i], ps_sem.at[1 + i, j], pr_sem.at[1 + i, j], to)))
 
@@ -402,11 +406,11 @@
         cols = slice(zz * 640, (zz + 1) * 640)
         piece = jnp.concatenate([b_rcv3[qq, :, zz * 80:(zz + 1) * 80].astype(F32) for qq in range(8)], axis=1)
         base[:, cols] = res[:, cols].astype(F32) + gb[:, cols] * piece
-    for j in range(5):
-        cols = slice(j * 1024, (j + 1) * 1024)
+    for j in range(2):
+        cols = slice(j * 2560, (j + 1) * 2560)
         for i in range(2):
             stage2[2 * j + i].wait_recv()
-        total = p_keep1[j, 0:32] + p_rcv1[j, 0:32].astype(F32) + p_rcv2[j].reshape(32, 1024).astype(F32)
+        total = p_keep1[j, 0:32] + p_rcv1[j, 0:32].astype(F32) + p_rcv2[j].reshape(32, 2560).astype(F32)
         mixed_out[:, cols] = (base[:, cols] + ga[:, cols] * total).astype(BF)
 
     for cp in sent:
@@ -440,8 +444,8 @@
             V((8, 80, 640), BF), V((2, 4, HD, 640), BF), V((2, 4, 2, 2, 32, 640), BF), V((2, 4, 2, 32, 640), BF),
             V((2, 4, 32, 640), BF), V((2, 4, 32, 640), F32), V((2, 4, 32, 640), BF), V((2, 4, 32, 640), BF), V((4, 32, 640), BF),
             V((8, 32, 640), BF), V((32, 5120), F32),
-            V((HD, 640), BF), V((HD, 5120), F32), V((5, 64, 1024), BF), V((5, 64, 1024), F32), V((5, 64, 1024), BF),
-            V((5, 2, 16, 1024), BF), V((5, 2, 16, 1024), BF),
+            V((HD, 640), BF), V((HD, 5120), F32), V((2, 64, 2560), BF), V((2, 64, 2560), F32), V((2, 64, 2560), BF),
+            V((2, 2, 16, 2560), BF), V((2, 2, 16, 2560), BF),
             D((9,)), D((4, 8)), D((4, 8)), D((4,)), D((4,)), D((3, 5, 2)), D((3, 5, 2)), D((4, 8)), D((4, 8)),
             D((10,)), D((10,)), D((5, 2)), D((5, 2)), D((8,)), D((8,)), D((11,)), D((11,)), D((3, 5)), D((3, 5)),
         ],

time: 73.2 us -> 73 us (level)
  no operation moved by 1% of the time
where the time goes in v6:
time: 73 us; the launch traced here: 72.9 us
  Pallas kernels  72.2 us (99%)
    pallas_call x1, Pallas kernels, window(): pl.pallas_call(window_kernel, out_shape=(jax.ShapeDtypeStruct((32, 5120),...  70.4 us
    pallas_call x1, Pallas kernels, finish(): pl.pallas_call(finish_kernel, out_shape=(jax.ShapeDtypeStruct(mixed.shape...  1.81 us

profile of v6, /device:TPU:1, one launch (start us, length us, event | category | flops | bytes accessed | tf_op | source)
XLA Modules:
  0.0 72.9 jit_solution(7468669947514188262)
XLA Ops:
  0.6 70.4 %window.1 = (bf16[32,5120]{1,0:T(8,128)(2,1)}, bf16[128,640]{1,0:T(8,128)(2,1)}) custom-call(bf16[32,2560]{1,0:T(8,128)(2,1)} %q_hbm.1, bf16[32,2560]{1,0:T(8,128)(2,1)} %k_hbm.1, bf16[32,2560]{1,0:T(8,128)(2,1)} %v_hbm.1, bf16[32,5120]{1,0:T(8,128)(2,1)} %res_hbm.1, bf16[128,640]{1,0:T(8,128)(2,1)} %ctx_hbm.1, bf16[640,5120]{1,0:T(8,128)(2,1)} %wa_hbm.1, ...), custom_call_target="tpu_custom_call" | custom-call | tf_op jit(solution)/shard_map/window/pallas_call | solution.py:429
  71.1 1.8 %finish.1 = (bf16[32,5120]{1,0:T(8,128)(2,1)}, bf16[128,640]{1,0:T(8,128)(2,1)}) custom-call(bf16[32,5120]{1,0:T(8,128)(2,1)} %get-tuple-element.4.mixed_in, bf16[128,640]{1,0:T(8,128)(2,1)} %get-tuple-element.5.cache_in), custom_call_target="tpu_custom_call" | custom-call | tf_op jit(solution)/shard_map/finish/pallas_call | solution.py:464
